TPU v7x, 32 devices: a whole 2x2x4 slice. The times are simulated.
32 devices in a mesh: gx: 16 (over z, x, core), gy: 2 (over y).
Axes of the slice: x: 2, y: 2, z: 4, core: 2. Of those that a mesh axis runs over, the one named last changes fastest.
Arguments:
- flow_populations: float32 [19, 32, 16, 256], P(None, 'gx', None, 'gy'), as said below
- heat_populations: float32 [7, 32, 16, 256], P(None, 'gx', None, 'gy'), as said below
- flow_weight: float32 [3, 32, 16, 256], P(None, 'gx', None, 'gy'), may hold values from -48 to 48
- heat_weight: float32 [32, 16, 256], P('gx', None, 'gy'), may hold values from -192 to 192
- resistance: float32 [32, 16, 256], P('gx', None, 'gy'), may hold values from 0.05 to 2
- conductivity: float32 [32, 16, 256], P('gx', None, 'gy'), may hold values from 0.5 to 2
- solid_mask: int32 [32, 16, 256], P('gx', None, 'gy'), may hold values 0 or 1
Outputs:
- resistance_sensitivity: float32 [32, 16, 256], P('gx', None, 'gy')
- conductivity_sensitivity: float32 [32, 16, 256], P('gx', None, 'gy')
Inputs may be any that keep to these rules, and one draw needn't show every extreme that they name: `solid_mask`: 1 marks a solid voxel, 0 a fluid one. `flow_populations`: positive. `heat_populations`: positive.
All inputs are finite; a program needn't handle non-finite values. No bound on the sum of `solid_mask` on one device may be relied on, other than what follows from the above.
Results may differ from a plain program's by a relative error of at most 0.0003.
Values sent between devices are 32-bit elements; how exact they have to be, the bound alone decides.
A program may use at most 64 MiB of HBM per device.

v0:
```python
import jax
import jax.numpy as jnp
import numpy as np
from jax import lax
from jax.sharding import PartitionSpec as P

STEPS = 3


GHOST_RATE = 1.2
HEAT_RATE = 1.4


def with_halo(block, sides, width):
    for axis, dim in sides:
        count = lax.axis_size(axis)
        forward = [(i, i + 1) for i in range(count - 1)]
        forward.append((count - 1, 0))
        backward = [(target, source) for source, target in forward]
        low = lax.ppermute(
            lax.slice_in_dim(block, block.shape[dim] - width, None, axis=dim), axis, forward
        )
        high = lax.ppermute(lax.slice_in_dim(block, 0, width, axis=dim), axis, backward)
        block = jnp.concatenate([low, block, high], axis=dim)
    return block


def lattice_tables():
    velocity = np.array(
        [
            [0, 0, 0],
            [1, 0, 0],
            [-1, 0, 0],
            [0, 1, 0],
            [0, -1, 0],
            [0, 0, 1],
            [0, 0, -1],
            [1, 1, 0],
            [-1, -1, 0],
            [1, -1, 0],
            [-1, 1, 0],
            [1, 0, 1],
            [-1, 0, -1],
            [1, 0, -1],
            [-1, 0, 1],
            [0, 1, 1],
            [0, -1, -1],
            [0, 1, -1],
            [0, -1, 1],
        ],
        np.int64,
    )
    weights = np.array([1.0 / 3.0] + [1.0 / 18.0] * 6 + [1.0 / 36.0] * 12, np.float32)
    energy_stencil_factors = np.array([0.25] + [0.125] * 6, np.float32)
    dot_table = (velocity @ velocity.T).astype(np.float32)
    lengths = np.sum(velocity * velocity, axis=1).astype(np.float32)
    stress_map = (4.5 * weights[:, None] * (dot_table * dot_table - lengths[None, :] / 3.0)).astype(
        np.float32
    )
    flux_map = (4.0 * energy_stencil_factors[:, None] * dot_table[:7, :7]).astype(np.float32)
    opposite = np.array([0, 2, 1, 4, 3, 6, 5, 8, 7, 10, 9, 12, 11, 14, 13, 16, 15, 18, 17])
    return (velocity, weights, energy_stencil_factors, stress_map, flux_map, opposite)


def full_velocity():
    velocity = lattice_tables()[0]
    return np.concatenate([velocity, velocity[:7]], axis=0)


def collide(flow_part, energy_share, resistance, conductivity, solid_cells):
    velocity, weights, energy_stencil_factors, stress_map, flux_map, opposite = lattice_tables()
    highest = lax.Precision.HIGHEST
    vel_float = velocity.astype(np.float32)
    momentum = jnp.einsum("qa,qxzy->axzy", vel_float, flow_part, precision=highest)
    density = jnp.sum(flow_part, axis=0)
    warmth_grid = jnp.sum(energy_share, axis=0)
    fluid_cells = 1.0 - solid_cells
    velocity_field = momentum * (fluid_cells / (1.0 + resistance))
    chosen_heading = jnp.einsum("qa,axzy->qxzy", vel_float, velocity_field, precision=highest)
    kinetic = jnp.sum(velocity_field * velocity_field, axis=0)
    equilibrium = weights[:, None, None, None] * (
        density + 3.0 * chosen_heading + 4.5 * chosen_heading * chosen_heading - 1.5 * kinetic
    )
    excess = flow_part - equilibrium
    stress = jnp.einsum("iq,qxzy->ixzy", stress_map, excess, precision=highest)
    momentum_diffusivity = 0.1 * jnp.exp(-2.0 * (warmth_grid - 1.0))
    shear_rate = 1.0 / (0.5 + 3.0 * momentum_diffusivity)
    relaxed = equilibrium + (1.0 - shear_rate) * stress + (1.0 - GHOST_RATE) * (excess - stress)
    bounced = flow_part[opposite]
    flow_post = solid_cells * bounced + fluid_cells * relaxed
    energy_balanced_populations = (
        energy_stencil_factors[:, None, None, None] * warmth_grid * (1.0 + 4.0 * chosen_heading[:7])
    )
    heat_excess = energy_share - energy_balanced_populations
    heat_flux = jnp.einsum("iq,qxzy->ixzy", flux_map, heat_excess, precision=highest)
    flux_rate = 1.0 / (0.5 + 0.4 * conductivity)
    heat_post = (
        energy_balanced_populations
        + (1.0 - flux_rate) * heat_flux
        + (1.0 - HEAT_RATE) * (heat_excess - heat_flux)
    )
    return (flow_post, heat_post)


def stream_rims(lattice_state, velocity_table):
    members_total = velocity_table.shape[0]
    padded = with_halo(lattice_state, (("gx", 1), ("gy", 3)), 1)
    width_x = lattice_state.shape[1]
    width_y = lattice_state.shape[3]
    shifted = []
    for member in range(members_total):
        step_x, step_y, step_z = (int(entry_value) for entry_value in velocity_table[member])
        window_cells = padded[
            member, 1 - step_x : 1 - step_x + width_x, :, 1 - step_y : 1 - step_y + width_y
        ]
        shifted.append(jnp.roll(window_cells, step_z, axis=1))
    return jnp.stack(shifted)


def stream_table(lattice_state, velocity_table):
    result_state = stream_rims(lattice_state, velocity_table)
    return result_state


def stream(lattice_state, direction):
    return stream_table(lattice_state, full_velocity() * direction)


def objective_seed(flow_weight, heat_weight):
    vel_float = lattice_tables()[0].astype(np.float32)
    flow_seed = jnp.einsum("qa,axzy->qxzy", vel_float, flow_weight, precision=lax.Precision.HIGHEST)
    heat_seed = jnp.broadcast_to(heat_weight[None], (7,) + heat_weight.shape)
    return jnp.concatenate([flow_seed, heat_seed], axis=0)


def on_device(
    flow_populations,
    heat_populations,
    flow_weight,
    heat_weight,
    resistance,
    conductivity,
    solid_mask,
):
    solid_cells = solid_mask.astype(jnp.float32)
    initial = jnp.concatenate([flow_populations, heat_populations], axis=0)

    def local_step(flow_part, energy_share, resist_field, conduct_field):
        return collide(flow_part, energy_share, resist_field, conduct_field, solid_cells)

    adjoint = objective_seed(flow_weight, heat_weight)
    resistance_sensitivity = jnp.zeros_like(resistance)
    conductivity_sensitivity = jnp.zeros_like(conductivity)
    history = [initial]
    for section_index in range(STEPS - 1):
        lattice_state = history[-1]
        flow_post, heat_post = collide(
            lattice_state[:19], lattice_state[19:], resistance, conductivity, solid_cells
        )
        history.append(stream(jnp.concatenate([flow_post, heat_post], axis=0), 1))
    for section_index in reversed(range(STEPS)):
        arrived = stream(adjoint, -1)
        saved_state = history[section_index]
        unused, pullback = jax.vjp(
            local_step, saved_state[:19], saved_state[19:], resistance, conductivity
        )
        flow_back, heat_back, resist_back, conduct_back = pullback((arrived[:19], arrived[19:]))
        adjoint, resist_back, conduct_back = (
            jnp.concatenate([flow_back, heat_back], axis=0),
            resist_back,
            conduct_back,
        )
        resistance_sensitivity = resistance_sensitivity + resist_back
        conductivity_sensitivity = conductivity_sensitivity + conduct_back
    return (resistance_sensitivity, conductivity_sensitivity)


def solution(mesh):
    placed = (
        P(None, "gx", None, "gy"),
        P(None, "gx", None, "gy"),
        P(None, "gx", None, "gy"),
        P("gx", None, "gy"),
        P("gx", None, "gy"),
        P("gx", None, "gy"),
        P("gx", None, "gy"),
    )
    return jax.shard_map(
        on_device,
        mesh=mesh,
        in_specs=placed,
        out_specs=(P("gx", None, "gy"), P("gx", None, "gy")),
        check_vma=False,
    )
```

profile of v0, /device:TPU:0, one launch (start us, length us, event | category | flops | bytes accessed | tf_op | source)
XLA Modules:
  0.0 161.0 jit_solution(4607798438930085362)
XLA Ops:
  0.7 0.8 copy-done
  3.3 5.0 %collective-permute-start.8 = (f32[26,1,16,128]{3,2,1,0:T(8,128)S(1)}, f32[26,1,16,128]{3,2,1,0:T(8,128)S(1)}, u32[]{:S(2)}, u32[]{:S(2)}) collective-permute-start(f32[26,1,16,128]{3,2,1,0:T(8,128)S(1)} %get-tuple-element.147), channel_id=1, source_target_pairs={{2,0},{4,2},{6,4},{8,6},{10,8},{12,10},{14,12},{16,14},{18,16},{20... | collective-permute-start | bytes 638984 | tf_op jit(solution)/shard_map/ppermute | solution.py:23
  8.4 0.7 copy-done.49
  9.2 0.7 copy-done.74
  16.2 0.8 fusion.57
  17.0 4.4 %collective-permute-start.1 = (f32[26,1,16,128]{3,2,1,0:T(8,128)}, f32[26,1,16,128]{3,2,1,0:T(8,128)S(1)}, u32[]{:S(2)}, u32[]{:S(2)}) collective-permute-start(f32[26,1,16,128]{3,2,1,0:T(8,128)} %get-tuple-element.145), channel_id=1, source_target_pairs={{2,0},{4,2},{6,4},{8,6},{10,8},{12,10},{14,12},{16,14},{18,16},{20... | collective-permute-start | bytes 638984 | tf_op jit(solution)/shard_map/ppermute | solution.py:23
  24.1 1.3 copy.793
  25.4 1.3 copy.791
  26.7 1.9 %collective-permute-start.10 = (f32[26,4,16,1]{0,2,3,1:T(8,128)}, f32[26,4,16,1]{0,2,3,1:T(8,128)}, u32[]{:S(2)}, u32[]{:S(2)}) collective-permute-start(f32[26,4,16,1]{0,2,3,1:T(8,128)} %copy.791), channel_id=1, source_target_pairs={{1,0},{0,1},{3,2},{2,3},{5,4},{4,5},{7,6},{6,7},{9,8},{8,9},{11,10... | collective-permute-start | bytes 19976 | tf_op jit(solution)/shard_map/ppermute | solution.py:23
  29.1 1.3 copy.766
  30.4 1.3 copy.768
  31.7 1.9 %collective-permute-start.3 = (f32[26,4,16,1]{0,2,3,1:T(8,128)}, f32[26,4,16,1]{0,2,3,1:T(8,128)}, u32[]{:S(2)}, u32[]{:S(2)}) collective-permute-start(f32[26,4,16,1]{0,2,3,1:T(8,128)} %copy.768), channel_id=1, source_target_pairs={{1,0},{0,1},{3,2},{2,3},{5,4},{4,5},{7,6},{6,7},{9,8},{8,9},{11,10... | collective-permute-start | bytes 19976 | tf_op jit(solution)/shard_map/ppermute | solution.py:23
  34.9 1.6 %copy.794 = f32[26,4,16,1]{3,2,1,0:T(8,128)S(1)} copy(f32[26,4,16,1]{0,2,3,1:T(8,128)} %collective-permute-done.11) | data formatting | bytes 13312 | tf_op jit(solution)/shard_map/ppermute | solution.py:20
  36.5 1.6 %copy.792 = f32[26,4,16,1]{3,2,1,0:T(8,128)S(1)} copy(f32[26,4,16,1]{0,2,3,1:T(8,128)} %collective-permute-done.10) | data formatting | bytes 13312 | tf_op jit(solution)/shard_map/ppermute | solution.py:23
  38.2 0.7 constant_dynamic-update-slice_fusion.60
  40.8 0.7 constant_dynamic-update-slice_fusion.56
  41.5 0.7 maximum_bitcast_fusion.21
  42.2 0.7 maximum_bitcast_fusion.16
  42.9 1.6 %copy.767 = f32[26,4,16,1]{3,2,1,0:T(8,128)S(1)} copy(f32[26,4,16,1]{0,2,3,1:T(8,128)} %collective-permute-done.2) | data formatting | bytes 13312 | tf_op jit(solution)/shard_map/ppermute | solution.py:20
  45.1 0.7 maximum_bitcast_fusion.17
  50.9 1.7 %copy.769 = f32[26,4,16,1]{3,2,1,0:T(8,128)S(1)} copy(f32[26,4,16,1]{0,2,3,1:T(8,128)} %collective-permute-done.3) | data formatting | bytes 13312 | tf_op jit(solution)/shard_map/ppermute | solution.py:23
  54.8 0.7 copy-done.37
  55.8 1.2 multiply_reduce_fusion.3
  57.0 0.7 gather_fusion.1
  57.7 1.3 fusion.102
  61.9 0.7 copy-done.66
  66.3 0.7 copy-done.72
  67.0 0.7 copy-done.23
  68.9 4.4 %collective-permute-start.5 = (f32[26,1,16,128]{3,2,1,0:T(8,128)S(1)}, f32[26,1,16,128]{3,2,1,0:T(8,128)S(1)}, u32[]{:S(2)}, u32[]{:S(2)}) collective-permute-start(f32[26,1,16,128]{3,2,1,0:T(8,128)S(1)} %get-tuple-element.143), channel_id=1, source_target_pairs={{2,0},{4,2},{6,4},{8,6},{10,8},{12,10},{14,12},{16,14},{18,16},{20... | collective-permute-start | bytes 638984 | tf_op jit(solution)/shard_map/ppermute | solution.py:23
  73.3 0.7 copy-done.69
  74.0 0.7 copy-done.68
  74.8 0.7 copy-done.65
  76.1 0.7 collective-permute-done.4
  77.2 1.3 copy.783
  78.5 1.9 %collective-permute-start.6 = (f32[26,4,16,1]{0,2,3,1:T(8,128)}, f32[26,4,16,1]{0,2,3,1:T(8,128)S(1)}, u32[]{:S(2)}, u32[]{:S(2)}) collective-permute-start(f32[26,4,16,1]{0,2,3,1:T(8,128)} %copy.783), channel_id=1, source_target_pairs={{0,1},{1,0},{2,3},{3,2},{4,5},{5,4},{6,7},{7,6},{8,9},{9,8},{10,11... | collective-permute-start | bytes 19976 | tf_op jit(solution)/shard_map/ppermute | solution.py:20
  80.4 0.7 constant_dynamic-update-slice_fusion.45
  82.6 0.9 copy.784
  83.5 0.7 maximum_bitcast_fusion.27
  90.0 1.6 %copy.786 = f32[26,4,16,1]{3,2,1,0:T(8,128)S(1)} copy(f32[26,4,16,1]{0,2,3,1:T(8,128)} %collective-permute-done.7) | data formatting | bytes 13312 | tf_op jit(solution)/shard_map/ppermute | solution.py:23
  91.8 0.7 copy-done.35
  93.4 0.8 copy-done.40
  94.2 0.7 copy-done.48
  95.8 0.8 copy-done.8
  102.2 1.1 multiply_reduce_fusion.5
  104.7 1.9 %scatter_fusion = f32[19,2,16,128]{3,2,1,0:T(8,128)S(1)} fusion(f32[19,2,16,128]{3,2,1,0:T(8,128)S(1)} %copy_add_fusion.3, s32[19]{0:T(128)S(1)} %copy-done.96, f32[19,2,16,128]{3,2,1,0:T(8,128)S(1)} %get-tuple-element.154), kind=kCustom, calls=%fused_computation.2 | custom fusion | flops 77824 | bytes 933964 | tf_op jit(solution)/shard_map/transpose(jvp())/scatter-add | solution.py:89
  106.7 4.4 %collective-permute-start.12 = (f32[26,1,16,128]{3,2,1,0:T(8,128)S(1)}, f32[26,1,16,128]{3,2,1,0:T(8,128)S(1)}, u32[]{:S(2)}, u32[]{:S(2)}) collective-permute-start(f32[26,1,16,128]{3,2,1,0:T(8,128)S(1)} %get-tuple-element.141), channel_id=1, source_target_pairs={{2,0},{4,2},{6,4},{8,6},{10,8},{12,10},{14,12},{16,14},{18,16},{20... | collective-permute-start | bytes 638984 | tf_op jit(solution)/shard_map/ppermute | solution.py:23
  111.1 3.5 %collective-permute-done.13 = f32[26,1,16,128]{3,2,1,0:T(8,128)S(1)} collective-permute-done((f32[26,1,16,128]{3,2,1,0:T(8,128)S(1)}, f32[26,1,16,128]{3,2,1,0:T(8,128)S(1)}, u32[]{:S(2)}, u32[]{:S(2)}) %collective-permute-start.13) | collective-permute-done | bytes 213024 | tf_op jit(solution)/shard_map/ppermute | solution.py:20
  116.4 1.9 %collective-permute-start.14 = (f32[26,4,16,1]{0,2,3,1:T(8,128)S(1)}, f32[26,4,16,1]{0,2,3,1:T(8,128)S(1)}, u32[]{:S(2)}, u32[]{:S(2)}) collective-permute-start(f32[26,4,16,1]{0,2,3,1:T(8,128)S(1)} %copy.818), channel_id=1, source_target_pairs={{1,0},{0,1},{3,2},{2,3},{5,4},{4,5},{7,6},{6,7},{9,8},{8,9},{11,10... | collective-permute-start | bytes 19976 | tf_op jit(solution)/shard_map/ppermute | solution.py:23
  118.5 3.8 %collective-permute-done.15 = f32[26,4,16,1]{0,2,3,1:T(8,128)S(1)} collective-permute-done((f32[26,4,16,1]{0,2,3,1:T(8,128)S(1)}, f32[26,4,16,1]{0,2,3,1:T(8,128)S(1)}, u32[]{:S(2)}, u32[]{:S(2)}) %collective-permute-start.15) | collective-permute-done | bytes 6688 | tf_op jit(solution)/shard_map/ppermute | solution.py:20
  122.2 0.9 copy.821
  123.1 0.9 copy.819
  124.8 0.7 copy-done.24
  127.1 0.7 copy-done.42
  129.0 0.7 copy-done.18
  132.4 0.8 copy-done.13
  133.2 1.1 fusion.91
  135.6 1.9 %scatter_fusion.1 = f32[19,2,16,128]{3,2,1,0:T(8,128)S(1)} fusion(f32[19,2,16,128]{3,2,1,0:T(8,128)S(1)} %copy_add_fusion.1, s32[19]{0:T(128)S(1)} %copy-done.97, f32[19,2,16,128]{3,2,1,0:T(8,128)S(1)} %get-tuple-element.150), kind=kCustom, calls=%fused_computation.3 | custom fusion | flops 77824 | bytes 933964 | tf_op jit(solution)/shard_map/transpose(jvp())/scatter-add | solution.py:89
  137.6 4.4 %collective-permute-start.16 = (f32[26,1,16,128]{3,2,1,0:T(8,128)S(1)}, f32[26,1,16,128]{3,2,1,0:T(8,128)S(1)}, u32[]{:S(2)}, u32[]{:S(2)}) collective-permute-start(f32[26,1,16,128]{3,2,1,0:T(8,128)S(1)} %get-tuple-element.139), channel_id=1, source_target_pairs={{2,0},{4,2},{6,4},{8,6},{10,8},{12,10},{14,12},{16,14},{18,16},{20... | collective-permute-start | bytes 638984 | tf_op jit(solution)/shard_map/ppermute | solution.py:23
  142.1 3.5 %collective-permute-done.17 = f32[26,1,16,128]{3,2,1,0:T(8,128)S(1)} collective-permute-done((f32[26,1,16,128]{3,2,1,0:T(8,128)S(1)}, f32[26,1,16,128]{3,2,1,0:T(8,128)S(1)}, u32[]{:S(2)}, u32[]{:S(2)}) %collective-permute-start.17) | collective-permute-done | bytes 213024 | tf_op jit(solution)/shard_map/ppermute | solution.py:20
  147.7 1.7 %collective-permute-start.19 = (f32[26,4,16,1]{0,2,3,1:T(8,128)S(1)}, f32[26,4,16,1]{0,2,3,1:T(8,128)S(1)}, u32[]{:S(2)}, u32[]{:S(2)}) collective-permute-start(f32[26,4,16,1]{0,2,3,1:T(8,128)S(1)} %copy.841), channel_id=1, source_target_pairs={{0,1},{1,0},{2,3},{3,2},{4,5},{5,4},{6,7},{7,6},{8,9},{9,8},{10,11... | collective-permute-start | bytes 19976 | tf_op jit(solution)/shard_map/ppermute | solution.py:20
  149.4 2.2 %collective-permute-done.19 = f32[26,4,16,1]{0,2,3,1:T(8,128)S(1)} collective-permute-done((f32[26,4,16,1]{0,2,3,1:T(8,128)S(1)}, f32[26,4,16,1]{0,2,3,1:T(8,128)S(1)}, u32[]{:S(2)}, u32[]{:S(2)}) %collective-permute-start.19) | collective-permute-done | bytes 6688 | tf_op jit(solution)/shard_map/ppermute | solution.py:20
  151.6 0.9 copy.842
  152.5 0.9 copy.840
  156.0 0.7 copy-done.44
  (519 shorter events, 64.7 us)
Async XLA Ops:
  0.6 0.8 copy-start
  0.6 0.8 copy-start.25
  2.7 5.6 %copy-start.63 = (f32[2,16,128]{2,1,0:T(8,128)S(1)}, f32[2,16,128]{2,1,0:T(8,128)}, u32[]{:S(2)}) copy-start(f32[2,16,128]{2,1,0:T(8,128)} %param.51) | copy-start | bytes 49156
  2.7 6.4 %copy-start.19 = (f32[7,2,16,128]{3,2,1,0:T(8,128)S(1)}, f32[7,2,16,128]{3,2,1,0:T(8,128)}, u32[]{:S(2)}) copy-start(f32[7,2,16,128]{3,2,1,0:T(8,128)} %param.47) | copy-start | bytes 344068
  2.7 6.4 %copy-start.1 = (f32[19,2,16,128]{3,2,1,0:T(8,128)S(1)}, f32[19,2,16,128]{3,2,1,0:T(8,128)}, u32[]{:S(2)}) copy-start(f32[19,2,16,128]{3,2,1,0:T(8,128)} %param.46) | copy-start | bytes 933892
  2.8 5.6 %copy-start.95 = (s32[19]{0:T(128)S(1)}, s32[19]{0:T(128)}, u32[]{:S(2)}) copy-start(s32[19]{0:T(128)} %constant.75) | copy-start | bytes 232
  2.8 21.0 %collective-permute-start.9 = (f32[26,1,16,128]{3,2,1,0:T(8,128)S(1)}, f32[26,1,16,128]{3,2,1,0:T(8,128)S(1)}, u32[]{:S(2)}, u32[]{:S(2)}) collective-permute-start(f32[26,1,16,128]{3,2,1,0:T(8,128)S(1)} %get-tuple-element.146), channel_id=1, source_target_pairs={{0,2},{2,4},{4,6},{6,8},{8,10},{10,12},{12,14},{14,16},{16,18},{18... | collective-permute-start | bytes 638984 | tf_op jit(solution)/shard_map/ppermute | solution.py:20
  3.3 20.5 %collective-permute-start.8 = (f32[26,1,16,128]{3,2,1,0:T(8,128)S(1)}, f32[26,1,16,128]{3,2,1,0:T(8,128)S(1)}, u32[]{:S(2)}, u32[]{:S(2)}) collective-permute-start(f32[26,1,16,128]{3,2,1,0:T(8,128)S(1)} %get-tuple-element.147), channel_id=1, source_target_pairs={{2,0},{4,2},{6,4},{8,6},{10,8},{12,10},{14,12},{16,14},{18,16},{20... | collective-permute-start | bytes 638984 | tf_op jit(solution)/shard_map/ppermute | solution.py:23
  8.4 2.0 %copy-start.94 = (s32[1024]{0:T(1024)}, s32[1024]{0:T(1024)S(1)}, u32[]{:S(2)}) copy-start(s32[1024]{0:T(1024)S(1)} %pad_clamp_fusion) | copy-start | bytes 12292
  9.1 6.2 %copy-start.22 = (f32[2,16,128]{2,1,0:T(8,128)}, f32[2,16,128]{2,1,0:T(8,128)S(1)}, u32[]{:S(2)}) copy-start(f32[2,16,128]{2,1,0:T(8,128)S(1)} %divide_subtract_fusion) | copy-start | bytes 49156
  9.1 6.1 %copy-start.20 = (f32[2,16,128]{2,1,0:T(8,128)}, f32[2,16,128]{2,1,0:T(8,128)S(1)}, u32[]{:S(2)}) copy-start(f32[2,16,128]{2,1,0:T(8,128)S(1)} %reduce_sum.445) | copy-start | bytes 49156
  11.6 4.3 %copy-start.43 = (f32[2,16,128]{2,1,0:T(8,128)}, f32[2,16,128]{2,1,0:T(8,128)S(1)}, u32[]{:S(2)}) copy-start(f32[2,16,128]{2,1,0:T(8,128)S(1)} %get-tuple-element.211) | copy-start | bytes 49156
  12.4 3.5 %copy-start.5 = (f32[19,2,16,128]{3,2,1,0:T(8,128)}, f32[19,2,16,128]{3,2,1,0:T(8,128)S(1)}, u32[]{:S(2)}) copy-start(f32[19,2,16,128]{3,2,1,0:T(8,128)S(1)} %get-tuple-element.49) | copy-start | bytes 933892
  17.0 11.8 %collective-permute-start = (f32[26,1,16,128]{3,2,1,0:T(8,128)}, f32[26,1,16,128]{3,2,1,0:T(8,128)S(1)}, u32[]{:S(2)}, u32[]{:S(2)}) collective-permute-start(f32[26,1,16,128]{3,2,1,0:T(8,128)} %get-tuple-element.144), channel_id=1, source_target_pairs={{0,2},{2,4},{4,6},{6,8},{8,10},{10,12},{12,14},{14,16},{16,18},{18... | collective-permute-start | bytes 638984 | tf_op jit(solution)/shard_map/ppermute | solution.py:20
  17.0 11.8 %collective-permute-start.1 = (f32[26,1,16,128]{3,2,1,0:T(8,128)}, f32[26,1,16,128]{3,2,1,0:T(8,128)S(1)}, u32[]{:S(2)}, u32[]{:S(2)}) collective-permute-start(f32[26,1,16,128]{3,2,1,0:T(8,128)} %get-tuple-element.145), channel_id=1, source_target_pairs={{2,0},{4,2},{6,4},{8,6},{10,8},{12,10},{14,12},{16,14},{18,16},{20... | collective-permute-start | bytes 638984 | tf_op jit(solution)/shard_map/ppermute | solution.py:23
  26.7 9.8 %collective-permute-start.10 = (f32[26,4,16,1]{0,2,3,1:T(8,128)}, f32[26,4,16,1]{0,2,3,1:T(8,128)}, u32[]{:S(2)}, u32[]{:S(2)}) collective-permute-start(f32[26,4,16,1]{0,2,3,1:T(8,128)} %copy.791), channel_id=1, source_target_pairs={{1,0},{0,1},{3,2},{2,3},{5,4},{4,5},{7,6},{6,7},{9,8},{8,9},{11,10... | collective-permute-start | bytes 19976 | tf_op jit(solution)/shard_map/ppermute | solution.py:23
  28.6 6.3 %collective-permute-start.11 = (f32[26,4,16,1]{0,2,3,1:T(8,128)}, f32[26,4,16,1]{0,2,3,1:T(8,128)}, u32[]{:S(2)}, u32[]{:S(2)}) collective-permute-start(f32[26,4,16,1]{0,2,3,1:T(8,128)} %copy.793), channel_id=1, source_target_pairs={{0,1},{1,0},{2,3},{3,2},{4,5},{5,4},{6,7},{7,6},{8,9},{9,8},{10,11... | collective-permute-start | bytes 19976 | tf_op jit(solution)/shard_map/ppermute | solution.py:20
  28.7 15.8 %copy-start.2 = (f32[26,1,16,128]{3,2,1,0:T(8,128)}, f32[26,1,16,128]{3,2,1,0:T(8,128)S(1)}, u32[]{:S(2)}) copy-start(f32[26,1,16,128]{3,2,1,0:T(8,128)S(1)} %collective-permute-done.1) | copy-start | bytes 638980
  31.7 19.3 %collective-permute-start.3 = (f32[26,4,16,1]{0,2,3,1:T(8,128)}, f32[26,4,16,1]{0,2,3,1:T(8,128)}, u32[]{:S(2)}, u32[]{:S(2)}) collective-permute-start(f32[26,4,16,1]{0,2,3,1:T(8,128)} %copy.768), channel_id=1, source_target_pairs={{1,0},{0,1},{3,2},{2,3},{5,4},{4,5},{7,6},{6,7},{9,8},{8,9},{11,10... | collective-permute-start | bytes 19976 | tf_op jit(solution)/shard_map/ppermute | solution.py:23
  33.6 9.3 %collective-permute-start.2 = (f32[26,4,16,1]{0,2,3,1:T(8,128)}, f32[26,4,16,1]{0,2,3,1:T(8,128)}, u32[]{:S(2)}, u32[]{:S(2)}) collective-permute-start(f32[26,4,16,1]{0,2,3,1:T(8,128)} %copy.766), channel_id=1, source_target_pairs={{0,1},{1,0},{2,3},{3,2},{4,5},{5,4},{6,7},{7,6},{8,9},{9,8},{10,11... | collective-permute-start | bytes 19976 | tf_op jit(solution)/shard_map/ppermute | solution.py:20
  45.1 9.6 %copy-start.36 = (f32[2,16,128]{2,1,0:T(8,128)}, f32[2,16,128]{2,1,0:T(8,128)S(1)}, u32[]{:S(2)}) copy-start(f32[2,16,128]{2,1,0:T(8,128)S(1)} %get-tuple-element.135) | copy-start | bytes 49156
  50.9 1.7 %copy-start.3 = (f32[26,1,16,128]{3,2,1,0:T(8,128)S(1)}, f32[26,1,16,128]{3,2,1,0:T(8,128)}, u32[]{:S(2)}) copy-start(f32[26,1,16,128]{3,2,1,0:T(8,128)} %copy-done.2) | copy-start | bytes 638980
  55.6 7.0 %copy-start.27 = (f32[2,16,128]{2,1,0:T(8,128)}, f32[2,16,128]{2,1,0:T(8,128)S(1)}, u32[]{:S(2)}) copy-start(f32[2,16,128]{2,1,0:T(8,128)S(1)} %get-tuple-element.39) | copy-start | bytes 49156
  57.0 2.0 %copy-start.12 = (f32[2,16,128,3]{2,3,1,0:T(4,128)}, f32[2,16,128,3]{2,3,1,0:T(4,128)S(1)}, u32[]{:S(2)}) copy-start(f32[2,16,128,3]{2,3,1,0:T(4,128)S(1)} %get-tuple-element.204) | copy-start | bytes 147460
  59.0 0.7 copy-start.54
  59.0 0.7 copy-start.51
  59.0 0.8 copy-start.52
  59.0 0.8 copy-start.99
  60.6 7.6 %copy-start.41 = (f32[2,16,128]{2,1,0:T(8,128)}, f32[2,16,128]{2,1,0:T(8,128)S(1)}, u32[]{:S(2)}) copy-start(f32[2,16,128]{2,1,0:T(8,128)S(1)} %get-tuple-element.31) | copy-start | bytes 49156
  61.9 2.1 %copy-start.17 = (f32[7,2,16,128]{3,2,1,0:T(8,128)}, f32[7,2,16,128]{3,2,1,0:T(8,128)S(1)}, u32[]{:S(2)}) copy-start(f32[7,2,16,128]{3,2,1,0:T(8,128)S(1)} %constant_dynamic-update-slice_fusion.19) | copy-start | bytes 344068
  64.6 1.0 copy-start.73
  65.3 0.9 copy-start.7
  68.7 4.6 %copy-start.4 = (f32[19,2,16,128]{3,2,1,0:T(8,128)S(1)}, f32[19,2,16,128]{3,2,1,0:T(8,128)}, u32[]{:S(2)}) copy-start(f32[19,2,16,128]{3,2,1,0:T(8,128)} %get-tuple-element.79) | copy-start | bytes 933892
  68.7 4.6 %copy-start.71 = (f32[2,15,128]{2,1,0:T(8,128)S(1)}, f32[2,15,128]{2,1,0:T(8,128)}, u32[]{:S(2)}) copy-start(f32[2,15,128]{2,1,0:T(8,128)} %slice.1297) | copy-start | bytes 46084
  68.8 8.0 %collective-permute-start.4 = (f32[26,1,16,128]{3,2,1,0:T(8,128)S(1)}, f32[26,1,16,128]{3,2,1,0:T(8,128)S(1)}, u32[]{:S(2)}, u32[]{:S(2)}) collective-permute-start(f32[26,1,16,128]{3,2,1,0:T(8,128)S(1)} %get-tuple-element.142), channel_id=1, source_target_pairs={{0,2},{2,4},{4,6},{6,8},{8,10},{10,12},{12,14},{14,16},{16,18},{18... | collective-permute-start | bytes 638984 | tf_op jit(solution)/shard_map/ppermute | solution.py:20
  68.8 4.4 %copy-start.103 = (f32[2,1,128]{2,1,0:T(1,128)S(1)}, f32[2,1,128]{2,1,0:T(1,128)}, u32[]{:S(2)}) copy-start(f32[2,1,128]{2,1,0:T(1,128)} %slice.1298) | copy-start | bytes 3076
  68.9 7.9 %collective-permute-start.5 = (f32[26,1,16,128]{3,2,1,0:T(8,128)S(1)}, f32[26,1,16,128]{3,2,1,0:T(8,128)S(1)}, u32[]{:S(2)}, u32[]{:S(2)}) collective-permute-start(f32[26,1,16,128]{3,2,1,0:T(8,128)S(1)} %get-tuple-element.143), channel_id=1, source_target_pairs={{2,0},{4,2},{6,4},{8,6},{10,8},{12,10},{14,12},{16,14},{18,16},{20... | collective-permute-start | bytes 638984 | tf_op jit(solution)/shard_map/ppermute | solution.py:23
  78.5 4.1 %collective-permute-start.6 = (f32[26,4,16,1]{0,2,3,1:T(8,128)}, f32[26,4,16,1]{0,2,3,1:T(8,128)S(1)}, u32[]{:S(2)}, u32[]{:S(2)}) collective-permute-start(f32[26,4,16,1]{0,2,3,1:T(8,128)} %copy.783), channel_id=1, source_target_pairs={{0,1},{1,0},{2,3},{3,2},{4,5},{5,4},{6,7},{7,6},{8,9},{9,8},{10,11... | collective-permute-start | bytes 19976 | tf_op jit(solution)/shard_map/ppermute | solution.py:20
  81.8 8.3 %collective-permute-start.7 = (f32[26,4,16,1]{0,2,3,1:T(8,128)S(1)}, f32[26,4,16,1]{0,2,3,1:T(8,128)}, u32[]{:S(2)}, u32[]{:S(2)}) collective-permute-start(f32[26,4,16,1]{0,2,3,1:T(8,128)S(1)} %copy.785), channel_id=1, source_target_pairs={{1,0},{0,1},{3,2},{2,3},{5,4},{4,5},{7,6},{6,7},{9,8},{8,9},{11,10... | collective-permute-start | bytes 19976 | tf_op jit(solution)/shard_map/ppermute | solution.py:23
  91.8 0.8 copy-start.86
  93.3 0.9 copy-start.40
  95.7 1.0 copy-start.8
  106.6 8.0 %collective-permute-start.13 = (f32[26,1,16,128]{3,2,1,0:T(8,128)S(1)}, f32[26,1,16,128]{3,2,1,0:T(8,128)S(1)}, u32[]{:S(2)}, u32[]{:S(2)}) collective-permute-start(f32[26,1,16,128]{3,2,1,0:T(8,128)S(1)} %get-tuple-element.140), channel_id=1, source_target_pairs={{0,2},{2,4},{4,6},{6,8},{8,10},{10,12},{12,14},{14,16},{16,18},{18... | collective-permute-start | bytes 638984 | tf_op jit(solution)/shard_map/ppermute | solution.py:20
  106.7 8.0 %collective-permute-start.12 = (f32[26,1,16,128]{3,2,1,0:T(8,128)S(1)}, f32[26,1,16,128]{3,2,1,0:T(8,128)S(1)}, u32[]{:S(2)}, u32[]{:S(2)}) collective-permute-start(f32[26,1,16,128]{3,2,1,0:T(8,128)S(1)} %get-tuple-element.141), channel_id=1, source_target_pairs={{2,0},{4,2},{6,4},{8,6},{10,8},{12,10},{14,12},{16,14},{18,16},{20... | collective-permute-start | bytes 638984 | tf_op jit(solution)/shard_map/ppermute | solution.py:23
  116.4 6.8 %collective-permute-start.14 = (f32[26,4,16,1]{0,2,3,1:T(8,128)S(1)}, f32[26,4,16,1]{0,2,3,1:T(8,128)S(1)}, u32[]{:S(2)}, u32[]{:S(2)}) collective-permute-start(f32[26,4,16,1]{0,2,3,1:T(8,128)S(1)} %copy.818), channel_id=1, source_target_pairs={{1,0},{0,1},{3,2},{2,3},{5,4},{4,5},{7,6},{6,7},{9,8},{8,9},{11,10... | collective-permute-start | bytes 19976 | tf_op jit(solution)/shard_map/ppermute | solution.py:23
  118.3 3.9 %collective-permute-start.15 = (f32[26,4,16,1]{0,2,3,1:T(8,128)S(1)}, f32[26,4,16,1]{0,2,3,1:T(8,128)S(1)}, u32[]{:S(2)}, u32[]{:S(2)}) collective-permute-start(f32[26,4,16,1]{0,2,3,1:T(8,128)S(1)} %copy.820), channel_id=1, source_target_pairs={{0,1},{1,0},{2,3},{3,2},{4,5},{5,4},{6,7},{7,6},{8,9},{9,8},{10,11... | collective-permute-start | bytes 19976 | tf_op jit(solution)/shard_map/ppermute | solution.py:20
  127.8 1.0 copy-start.9
  127.8 1.0 copy-start.79
  128.8 0.9 copy-start.18
  129.7 0.7 copy-start.60
  132.3 0.8 copy-start.13
  137.6 8.0 %collective-permute-start.17 = (f32[26,1,16,128]{3,2,1,0:T(8,128)S(1)}, f32[26,1,16,128]{3,2,1,0:T(8,128)S(1)}, u32[]{:S(2)}, u32[]{:S(2)}) collective-permute-start(f32[26,1,16,128]{3,2,1,0:T(8,128)S(1)} %get-tuple-element.138), channel_id=1, source_target_pairs={{0,2},{2,4},{4,6},{6,8},{8,10},{10,12},{12,14},{14,16},{16,18},{18... | collective-permute-start | bytes 638984 | tf_op jit(solution)/shard_map/ppermute | solution.py:20
  137.6 8.0 %collective-permute-start.16 = (f32[26,1,16,128]{3,2,1,0:T(8,128)S(1)}, f32[26,1,16,128]{3,2,1,0:T(8,128)S(1)}, u32[]{:S(2)}, u32[]{:S(2)}) collective-permute-start(f32[26,1,16,128]{3,2,1,0:T(8,128)S(1)} %get-tuple-element.139), channel_id=1, source_target_pairs={{2,0},{4,2},{6,4},{8,6},{10,8},{12,10},{14,12},{16,14},{18,16},{20... | collective-permute-start | bytes 638984 | tf_op jit(solution)/shard_map/ppermute | solution.py:23
  147.3 5.2 %collective-permute-start.18 = (f32[26,4,16,1]{0,2,3,1:T(8,128)S(1)}, f32[26,4,16,1]{0,2,3,1:T(8,128)S(1)}, u32[]{:S(2)}, u32[]{:S(2)}) collective-permute-start(f32[26,4,16,1]{0,2,3,1:T(8,128)S(1)} %copy.839), channel_id=1, source_target_pairs={{1,0},{0,1},{3,2},{2,3},{5,4},{4,5},{7,6},{6,7},{9,8},{8,9},{11,10... | collective-permute-start | bytes 19976 | tf_op jit(solution)/shard_map/ppermute | solution.py:23
  147.7 3.9 %collective-permute-start.19 = (f32[26,4,16,1]{0,2,3,1:T(8,128)S(1)}, f32[26,4,16,1]{0,2,3,1:T(8,128)S(1)}, u32[]{:S(2)}, u32[]{:S(2)}) collective-permute-start(f32[26,4,16,1]{0,2,3,1:T(8,128)S(1)} %copy.841), channel_id=1, source_target_pairs={{0,1},{1,0},{2,3},{3,2},{4,5},{5,4},{6,7},{7,6},{8,9},{9,8},{10,11... | collective-permute-start | bytes 19976 | tf_op jit(solution)/shard_map/ppermute | solution.py:20
  154.9 0.9 copy-start.11
  154.9 0.9 copy-start.21
  154.9 0.9 copy-start.85
  156.8 1.0 copy-start.6
  158.1 0.8 copy-start.16
  158.1 1.4 copy-start.61
  158.1 1.4 copy-start.64
  159.6 0.8 copy-start.70
  159.6 0.8 copy-start.75
  (62 other events, 43.2 us)
where the time goes:
time: 164 us; the launch traced here: 161 us
  local copies, waits for them, and re-layouts  71.7 us (44%)
  starting transfers between devices  33.7 us (21%)
  other arithmetic  22.1 us (13%)
  matrix products  16.1 us (10%)
  waiting for transfers between devices  14.4 us (9%)
  between operations  3 us (2%)
    unnamed x242, local copies, waits for them, and re-layouts  32.8 us
    ppermute x10, starting transfers between devices, with_halo(): lax.ppermute(lax.slice_in_dim(block, 0, width, axis=dim), axis, backward)  29.1 us
    ppermute x10, waiting for transfers between devices, with_halo(): lax.ppermute(lax.slice_in_dim(block, block.shape[dim] - width, None, axis...  14.4 us
    slice x91, local copies, waits for them, and re-layouts, stream_rims(): shifted.append(jnp.roll(window_cells, step_z, axis=1))  13.8 us
    ppermute x5, local copies, waits for them, and re-layouts, with_halo(): lax.ppermute(lax.slice_in_dim(block, 0, width, axis=dim), axis, backward)  6.71 us
    slice x10, local copies, waits for them, and re-layouts, with_halo(): lax.slice_in_dim(block, block.shape[dim] - width, None, axis=dim)  6.68 us
    ppermute x5, local copies, waits for them, and re-layouts, with_halo(): lax.ppermute(lax.slice_in_dim(block, block.shape[dim] - width, None, axis...  5.91 us
    dot_general x7, matrix products, collide(): jnp.einsum('qa,axzy->qxzy', vel_float, velocity_field, precision=highest)  5.72 us
  transfers between devices with their start and end apart: 20, of which 6 were waited for; matrix products, arithmetic and copies ran while one was open for 25% of the time, Pallas kernels for 0%

commit v1 on v0

v1 whole, which is shorter than its diff:
```python
import functools

import jax
import jax.numpy as jnp
from jax import lax
from jax.experimental import pallas as pl
from jax.experimental.pallas import tpu as pltpu
from jax.sharding import PartitionSpec as P

STEPS = 3
GHOST = 0.2
HEAT_GHOST = 0.4

FLOW = [
    (0, 0, 0), (1, 0, 0), (-1, 0, 0), (0, 1, 0), (0, -1, 0), (0, 0, 1), (0, 0, -1),
    (1, 1, 0), (-1, -1, 0), (1, -1, 0), (-1, 1, 0), (1, 0, 1), (-1, 0, -1),
    (1, 0, -1), (-1, 0, 1), (0, 1, 1), (0, -1, -1), (0, 1, -1), (0, -1, 1),
]
VELOCITY = FLOW + FLOW[:7]
MEMBERS = len(VELOCITY)
OPPOSITE = [0] + [q + 1 if q % 2 else q - 1 for q in range(1, 19)]
OPPOSITE = OPPOSITE + [19 + q for q in OPPOSITE[:7]]
ORDER = (
    [q for q in range(MEMBERS) if VELOCITY[q][0] == 1]
    + [q for q in range(MEMBERS) if VELOCITY[q][0] == -1]
    + [q for q in range(MEMBERS) if VELOCITY[q][0] == 0]
)
SLOT = [ORDER.index(q) for q in range(MEMBERS)]
FACE = sum(1 for q in range(MEMBERS) if VELOCITY[q][0] == 1)
UP = [q for q in range(MEMBERS) if VELOCITY[q][1] == 1]
DOWN = [q for q in range(MEMBERS) if VELOCITY[q][1] == -1]
ROUNDS = 5
FORWARD_0, SEED, FORWARD_1, BACK_2, BACK_1 = range(ROUNDS)
MESH = pl.DeviceIdType.MESH


def flow_moments(f):
    s = {q: f[q] + f[q + 1] for q in range(1, 19, 2)}
    d = {q: f[q] - f[q + 1] for q in range(1, 19, 2)}
    xy, xz, yz = s[7] + s[9], s[11] + s[13], s[15] + s[17]
    total = (f[0] + s[1] + s[3]) + (s[5] + xy) + (xz + yz)
    first = (
        (d[1] + d[7]) + (d[9] + d[11]) + d[13],
        (d[3] + d[7]) + (d[15] - d[9]) + d[17],
        (d[5] + d[11]) + (d[15] - d[13]) - d[17],
    )
    second = (
        s[1] + (xy + xz), s[3] + (xy + yz), s[5] + (xz + yz),
        s[7] - s[9], s[11] - s[13], s[15] - s[17],
    )
    return total, first, second


def spread(even, vector, tensor):
    x, y, z = vector
    xx, yy, zz, xy, xz, yz = tensor
    out = [even]

    def pair(e, o):
        out.append(e + o)
        out.append(e - o)

    ex, ey, ez = even + xx, even + yy, even + zz
    pair(ex, x)
    pair(ey, y)
    pair(ez, z)
    for e, cross, first, second in (
        (ex + yy, xy + xy, x, y), (ex + zz, xz + xz, x, z), (ey + zz, yz + yz, y, z)
    ):
        pair(e + cross, first + second)
        pair(e - cross, first - second)
    return out


def dot(a, b):
    return (a[0] * b[0] + a[1] * b[1]) + a[2] * b[2]


def state_moments(f, g, slow):
    density, momentum, second = flow_moments(f)
    third = density * (1.0 / 3.0)
    stress = tuple(m - third for m in second[:3]) + second[3:]
    u = tuple(slow * m for m in momentum)
    heat = (g[0] + (g[1] + g[2])) + ((g[3] + g[4]) + (g[5] + g[6]))
    flux = (g[1] - g[2], g[3] - g[4], g[5] - g[6])
    ease = jnp.exp(-2.0 * (heat - 1.0))
    omega = 1.0 / (0.5 + 0.3 * ease)
    return density, u, stress, heat, flux, omega, ease


def collide(f, g, solid, kappa, moments):
    density, u, stress, heat, flux, omega, _ = moments
    k_u, k_s = 4.5 * omega, 4.5 * (1.2 - omega)
    ku = tuple(k_u * m for m in u)
    tensor = (
        ku[0] * u[0] + k_s * stress[0], ku[1] * u[1] + k_s * stress[1],
        ku[2] * u[2] + k_s * stress[2], ku[0] * u[1] + k_s * stress[3],
        ku[0] * u[2] + k_s * stress[4], ku[1] * u[2] + k_s * stress[5],
    )
    even = 1.2 * density - (tensor[0] + tensor[1] + tensor[2]) * (1.0 / 3.0)
    vector = tuple(3.6 * m for m in u)
    w = 1.0 / 36.0
    relaxed = spread(
        w * even, tuple(w * m for m in vector), tuple(w * m for m in tensor)
    )
    out = []
    for q in range(19):
        scale = 12.0 if q == 0 else 2.0 if q < 7 else 1.0
        fluid = (relaxed[q] if scale == 1.0 else scale * relaxed[q]) - GHOST * f[q]
        out.append(jnp.where(solid, f[OPPOSITE[q]], fluid))
    sigma, pull = 1.4 - kappa, kappa * heat
    gate = tuple(0.5 * (pull * a + sigma * b) for a, b in zip(u, flux))
    base = (1.4 / 8.0) * heat
    out.append(2.0 * base - HEAT_GHOST * g[0])
    for axis in range(3):
        a, b = g[1 + 2 * axis], g[2 + 2 * axis]
        out.append((base + gate[axis]) - HEAT_GHOST * a)
        out.append((base - gate[axis]) - HEAT_GHOST * b)
    return out


def adjoint_sums(l, m, fluid):
    weighted = [12.0 * l[0]] + [2.0 * v for v in l[1:7]] + list(l[7:19])
    even, vector, tensor = flow_moments(weighted)
    scale = fluid * (1.0 / 36.0)
    even = scale * even
    vector = tuple(scale * v for v in vector)
    third = even * (1.0 / 3.0)
    tensor = tuple(scale * v - third for v in tensor[:3]) + tuple(scale * v for v in tensor[3:])
    gate = tuple(0.5 * (m[1 + 2 * k] - m[2 + 2 * k]) for k in range(3))
    return even, vector, tensor, gate


def sensitivities(sums, u, heat, flux, omega, kappa):
    _, vector, (xx, yy, zz, xy, xz, yz), gate = sums
    bent = (
        (xx * u[0] + xy * u[1]) + xz * u[2],
        (xy * u[0] + yy * u[1]) + yz * u[2],
        (xz * u[0] + yz * u[1]) + zz * u[2],
    )
    k_u, pull = 9.0 * omega, kappa * heat
    back = tuple(k_u * b + (3.6 * v + pull * e) for b, v, e in zip(bent, vector, gate))
    resist = dot(u, back)
    conduct = dot(gate, tuple(heat * a - b for a, b in zip(u, flux)))
    return back, bent, resist, conduct


def collide_back(l, m, sums, moments, back, bent, solid, slow, kappa):
    even, vector, tensor, gate = sums
    _, u, stress, heat, flux, omega, ease = moments
    xx, yy, zz, xy, xz, yz = tensor
    cross = xy * stress[3] + xz * stress[4] + yz * stress[5]
    inner = (xx * stress[0] + yy * stress[1]) + (zz * stress[2] + (cross + cross))
    omega_back = 4.5 * (dot(u, bent) - inner)
    k_s = 4.5 * (1.2 - omega)
    stress_back = tuple(k_s * t for t in tensor)
    density_back = 1.2 * even - (stress_back[0] + stress_back[1] + stress_back[2]) * (1.0 / 3.0)
    momentum_back = tuple(slow * b for b in back)
    smooth = spread(density_back, momentum_back, stress_back)
    out = []
    for q in range(19):
        out.append(jnp.where(solid, l[OPPOSITE[q]], -GHOST * l[q]) + smooth[q])
    moved = (m[0] + m[0] + (m[1] + m[2])) + ((m[3] + m[4]) + (m[5] + m[6]))
    heat_back = (1.4 / 8.0) * moved + kappa * dot(gate, u) + omega_back * (0.6 * ease) * (omega * omega)
    sigma = 1.4 - kappa
    flux_back = tuple(sigma * e for e in gate)
    out.append(heat_back - HEAT_GHOST * m[0])
    for axis in range(3):
        a, b = m[1 + 2 * axis], m[2 + 2 * axis]
        out.append((heat_back + flux_back[axis]) - HEAT_GHOST * a)
        out.append((heat_back - flux_back[axis]) - HEAT_GHOST * b)
    return out


def kernel(
    gx, gy, flow_ref, heat_ref, flow_w_ref, heat_w_ref, resist_ref, conduct_ref, solid_ref,
    resist_out, conduct_out,
    ext, own_edge, edge, saved, fields, send_sem, recv_sem,
):
    width, height, depth = resist_ref.shape
    sides = edge.shape[1]
    me_x, me_y = lax.axis_index("gx"), lax.axis_index("gy")
    right, left = lax.rem(me_x + 1, gx), lax.rem(me_x + gx - 1, gx)
    up, down = lax.rem(me_y + 1, gy), lax.rem(me_y + gy - 1, gy)
    columns = [(up, 0)] if sides == 1 else [(up, 0), (down, 1)]

    barrier = pltpu.get_barrier_semaphore()
    partners = [(right, me_y), (left, me_y)]
    for y, _ in columns:
        partners += [(me_x, y), (right, y), (left, y)]
    for partner in partners:
        pl.semaphore_signal(barrier, inc=1, device_id=partner, device_id_type=MESH)

    lane = lax.broadcasted_iota(jnp.int32, (height, depth), 1)

    def copies(r):
        made = []

        def add(src, dst, device):
            k = len(made)
            made.append(
                pltpu.make_async_remote_copy(
                    src_ref=src, dst_ref=dst,
                    send_sem=send_sem.at[r, k], recv_sem=recv_sem.at[r, k],
                    device_id=device, device_id_type=MESH,
                )
            )

        for y, side in columns:
            add(own_edge.at[r, width - 1], edge.at[r, side, 0], (right, y))
            add(own_edge.at[r, 0], edge.at[r, side, width + 1], (left, y))
        add(ext.at[r, width, pl.ds(0, FACE)], ext.at[r, 0, pl.ds(0, FACE)], (right, me_y))
        add(ext.at[r, 1, pl.ds(FACE, FACE)], ext.at[r, width + 1, pl.ds(FACE, FACE)], (left, me_y))
        for y, side in columns:
            add(own_edge.at[r], edge.at[r, side, pl.ds(1, width)], (me_x, y))
        return made

    def start(r):
        for copy in copies(r):
            copy.start()

    def arrive(r):
        for copy in copies(r):
            copy.wait_recv()

    def leave(r, x, members):
        packed = None
        for q in range(MEMBERS):
            if members[q] is None:
                continue
            value = members[q]
            _, step_y, step_z = VELOCITY[q]
            if step_z:
                value = pltpu.roll(value, step_z % height, 0)
            if step_y:
                value = pltpu.roll(value, step_y % depth, 1)
            ext[r, x + 1, SLOT[q]] = value
            if step_y:
                place = UP.index(q) if step_y == 1 else DOWN.index(q)
                shift = place * step_y % depth
                where = place if step_y == 1 else depth - 1 - place
                turned = pltpu.roll(value, shift, 1) if shift else value
                packed = turned if packed is None else jnp.where(lane == where, turned, packed)
        own_edge[r, x] = packed

    def gather(r, x, q):
        step_x, step_y, _ = VELOCITY[q]
        value = ext[r, x + 1 - step_x, SLOT[q]]
        if step_y:
            side = 0 if step_y == 1 else sides - 1
            packed = edge[r, side, x + 1 - step_x]
            place = UP.index(q) if step_y == 1 else DOWN.index(q)
            shift = -place * step_y % depth
            turned = pltpu.roll(packed, shift, 1) if shift else packed
            value = jnp.where(lane == (0 if step_y == 1 else depth - 1), turned, value)
        return value

    def keep(t, x, moments):
        _, u, stress, heat, flux, omega, ease = moments
        for k, value in enumerate((*u, heat, *flux, omega, ease, *stress)):
            saved[t, x, k] = value

    def kept(t, x, whole):
        values = [saved[t, x, k] for k in range(15 if whole else 8)]
        return (
            None, tuple(values[:3]), tuple(values[9:15]) if whole else None, values[3],
            tuple(values[4:7]), values[7], values[8] if whole else None,
        )

    def planes(body):
        def step(x, carry):
            body(x)
            return carry

        lax.fori_loop(0, width, step, 0)

    def first(x):
        solid = solid_ref[x] != 0
        slow = jnp.where(solid, 0.0, 1.0) / (1.0 + resist_ref[x])
        kappa = 1.0 / (0.5 + 0.4 * conduct_ref[x])
        fields[x, 0] = slow
        fields[x, 1] = kappa
        f = [flow_ref[q, x] for q in range(19)]
        g = [heat_ref[q, x] for q in range(7)]
        moments = state_moments(f, g, slow)
        keep(0, x, moments)
        leave(FORWARD_0, x, collide(f, g, solid, kappa, moments))

    planes(first)
    pl.semaphore_wait(barrier, len(partners))
    start(FORWARD_0)

    def seed(x):
        weights = [flow_w_ref[k, x] for k in range(3)]
        heat = heat_w_ref[x]
        members = [None] * MEMBERS
        for q in range(MEMBERS):
            if q >= 19:
                members[OPPOSITE[q]] = heat
            elif q:
                value = None
                for weight, step in zip(weights, VELOCITY[q]):
                    if step:
                        term = weight if step == 1 else -weight
                        value = term if value is None else value + term
                members[OPPOSITE[q]] = value
        leave(SEED, x, members)

    planes(seed)
    start(SEED)

    def second(x):
        solid, slow, kappa = solid_ref[x] != 0, fields[x, 0], fields[x, 1]
        state = [gather(FORWARD_0, x, q) for q in range(MEMBERS)]
        f, g = state[:19], state[19:]
        moments = state_moments(f, g, slow)
        keep(1, x, moments)
        leave(FORWARD_1, x, collide(f, g, solid, kappa, moments))

    arrive(FORWARD_0)
    planes(second)
    start(FORWARD_1)

    def reverse(r, x, moments, target):
        solid, slow, kappa = solid_ref[x] != 0, fields[x, 0], fields[x, 1]
        back = [
            jnp.zeros((height, depth), jnp.float32) if r == SEED and q == 0
            else gather(r, x, OPPOSITE[q])
            for q in range(MEMBERS)
        ]
        l, m = back[:19], back[19:]
        sums = adjoint_sums(l, m, jnp.where(solid, 0.0, 1.0))
        _, u, _, heat, flux, omega, _ = moments
        u_back, bent, resist, conduct = sensitivities(sums, u, heat, flux, omega, kappa)
        if r == SEED:
            resist_out[x] = resist
            conduct_out[x] = conduct
        elif target is not None:
            resist_out[x] += resist
            conduct_out[x] += conduct
        else:
            resist_out[x] = -(resist_out[x] + resist) / (1.0 + resist_ref[x])
            conduct_out[x] = (conduct_out[x] + conduct) * (-0.4 * kappa * kappa)
        if target is not None:
            out = collide_back(l, m, sums, moments, u_back, bent, solid, slow, kappa)
            leave(target, x, [out[OPPOSITE[q]] for q in range(MEMBERS)])

    def third(x):
        state = [gather(FORWARD_1, x, q) for q in range(MEMBERS)]
        reverse(SEED, x, state_moments(state[:19], state[19:], fields[x, 0]), BACK_2)

    arrive(SEED)
    arrive(FORWARD_1)
    planes(third)
    start(BACK_2)

    arrive(BACK_2)
    planes(lambda x: reverse(BACK_2, x, kept(1, x, True), BACK_1))
    start(BACK_1)

    arrive(BACK_1)
    planes(lambda x: reverse(BACK_1, x, kept(0, x, False), None))

    for r in range(ROUNDS):
        for copy in copies(r):
            copy.wait_send()


def on_device(gx, gy, flow, heat, flow_weight, heat_weight, resistance, conductivity, solid_mask):
    shape = resistance.shape
    width, height, depth = shape
    sides = 1 if gy == 2 else 2
    count = 2 + 3 * sides
    block = pl.BlockSpec(memory_space=pltpu.VMEM)
    return pl.pallas_call(
        functools.partial(kernel, gx, gy),
        out_shape=[jax.ShapeDtypeStruct(shape, jnp.float32)] * 2,
        in_specs=[block] * 7,
        out_specs=[block] * 2,
        scratch_shapes=[
            pltpu.VMEM((ROUNDS, width + 2, MEMBERS, height, depth), jnp.float32),
            pltpu.VMEM((ROUNDS, width, height, depth), jnp.float32),
            pltpu.VMEM((ROUNDS, sides, width + 2, height, depth), jnp.float32),
            pltpu.VMEM((STEPS - 1, width, 15, height, depth), jnp.float32),
            pltpu.VMEM((width, 2, height, depth), jnp.float32),
            pltpu.SemaphoreType.DMA((ROUNDS, count)),
            pltpu.SemaphoreType.DMA((ROUNDS, count)),
        ],
        compiler_params=pltpu.CompilerParams(
            collective_id=0, has_side_effects=True, vmem_limit_bytes=32 * 1024 * 1024
        ),
    )(flow, heat, flow_weight, heat_weight, resistance, conductivity, solid_mask)


def solution(mesh):
    wide, flat = P(None, "gx", None, "gy"), P("gx", None, "gy")
    return jax.shard_map(
        functools.partial(on_device, mesh.shape["gx"], mesh.shape["gy"]),
        mesh=mesh,
        in_specs=(wide, wide, wide, flat, flat, flat, flat),
        out_specs=(flat, flat),
        check_vma=False,
    )
```

time: 164 us -> 33.2 us (0.20); the launches traced: 161 us -> 32.7 us
  local copies, waits for them, and re-layouts: 71.7 us -> 6.74 us
  starting transfers between devices: 33.7 us -> 0 us
  Pallas kernels: 0 us -> 25.3 us
  other arithmetic: 22.1 us -> 0 us
  matrix products: 16.1 us -> 0 us
  waiting for transfers between devices: 14.4 us -> 0 us
  between operations: 3 us -> 0.66 us
    ppermute x20 -> x0, starting transfers between devices: 33.7 us -> none  [the longest x10 29.1 us: with_halo(): lax.ppermute(lax.slice_in_dim(block, 0, width, axis=dim), axis, backward)]
    unnamed x242 -> x16, local copies, waits for them, and re-layouts: 32.8 us -> 6.74 us
    pallas_call x0 -> x1, Pallas kernels: none -> 25.3 us  [on_device(): pl.pallas_call(functools.partial(kernel, gx, gy), out_shape=[jax.ShapeDty...]
    slice x106 -> x0, local copies, waits for them, and re-layouts: 25 us -> none  [the longest x91 13.8 us: stream_rims(): shifted.append(jnp.roll(window_cells, step_z, axis=1))]
    dot_general x27 -> x0, matrix products: 16.1 us -> none  [the longest x7 5.72 us: collide(): jnp.einsum('qa,axzy->qxzy', vel_float, velocity_field, precision=highest)]
    ppermute x20 -> x0, waiting for transfers between devices: 14.4 us -> none  [the longest x10 14.4 us: with_halo(): lax.ppermute(lax.slice_in_dim(block, block.shape[dim] - width, None, axis...]
    ppermute x10 -> x0, local copies, waits for them, and re-layouts: 12.6 us -> none  [the longest x5 6.71 us: with_halo(): lax.ppermute(lax.slice_in_dim(block, 0, width, axis=dim), axis, backward)]
    unnamed x65 -> x0, other arithmetic: 5.36 us -> none
  transfers between devices with their start and end apart: 20 -> 0, of which waited for: 6 -> 0; matrix products, arithmetic and copies ran while one was open for 25% -> 0% of each run, Pallas kernels for 0% -> 0%
where the time goes in v1:
time: 33.2 us; the launch traced here: 32.7 us
  Pallas kernels  25.3 us (76%)
  local copies, waits for them, and re-layouts  6.74 us (20%)
  between operations  0.66 us (2%)
    pallas_call x1, Pallas kernels, on_device(): pl.pallas_call(functools.partial(kernel, gx, gy), out_shape=[jax.ShapeDty...  25.3 us
    unnamed x16, local copies, waits for them, and re-layouts  6.74 us

profile of v1, /device:TPU:0, one launch (start us, length us, event | category | flops | bytes accessed | tf_op | source)
XLA Modules:
  0.0 32.7 jit_solution(10635391402972619228)
XLA Ops:
  0.6 0.0 copy-start
  0.6 1.0 %copy-done = f32[19,2,16,128]{3,2,1,0:T(8,128)S(1)} copy-done((f32[19,2,16,128]{3,2,1,0:T(8,128)S(1)}, f32[19,2,16,128]{3,2,1,0:T(8,128)}, u32[]{:S(2)}) %copy-start) | copy-done | bytes 311320
  1.6 0.0 copy-start.1
  1.6 0.9 %copy-done.1 = f32[7,2,16,128]{3,2,1,0:T(8,128)S(1)} copy-done((f32[7,2,16,128]{3,2,1,0:T(8,128)S(1)}, f32[7,2,16,128]{3,2,1,0:T(8,128)}, u32[]{:S(2)}) %copy-start.1) | copy-done | bytes 114712
  2.5 0.0 copy-start.2
  2.5 0.8 %copy-done.2 = f32[3,2,16,128]{3,2,1,0:T(8,128)S(1)} copy-done((f32[3,2,16,128]{3,2,1,0:T(8,128)S(1)}, f32[3,2,16,128]{3,2,1,0:T(8,128)}, u32[]{:S(2)}) %copy-start.2) | copy-done | bytes 49176
  3.3 0.0 copy-start.3
  3.3 0.7 %copy-done.3 = f32[2,16,128]{2,1,0:T(8,128)S(1)} copy-done((f32[2,16,128]{2,1,0:T(8,128)S(1)}, f32[2,16,128]{2,1,0:T(8,128)}, u32[]{:S(2)}) %copy-start.3) | copy-done | bytes 16408
  4.0 0.0 copy-start.4
  4.0 0.7 %copy-done.4 = f32[2,16,128]{2,1,0:T(8,128)S(1)} copy-done((f32[2,16,128]{2,1,0:T(8,128)S(1)}, f32[2,16,128]{2,1,0:T(8,128)}, u32[]{:S(2)}) %copy-start.4) | copy-done | bytes 16408
  4.7 0.0 copy-start.5
  4.7 0.7 %copy-done.5 = f32[2,16,128]{2,1,0:T(8,128)S(1)} copy-done((f32[2,16,128]{2,1,0:T(8,128)S(1)}, f32[2,16,128]{2,1,0:T(8,128)}, u32[]{:S(2)}) %copy-start.5) | copy-done | bytes 16408
  5.5 0.0 copy-start.6
  5.5 0.7 %copy-done.6 = s32[2,16,128]{2,1,0:T(8,128)S(1)} copy-done((s32[2,16,128]{2,1,0:T(8,128)S(1)}, s32[2,16,128]{2,1,0:T(8,128)}, u32[]{:S(2)}) %copy-start.6) | copy-done | bytes 16408
  6.2 25.3 %shard_map.86 = (f32[2,16,128]{2,1,0:T(8,128)S(1)}, f32[2,16,128]{2,1,0:T(8,128)S(1)}) custom-call(f32[19,2,16,128]{3,2,1,0:T(8,128)S(1)} %copy-done, f32[7,2,16,128]{3,2,1,0:T(8,128)S(1)} %copy-done.1, f32[3,2,16,128]{3,2,1,0:T(8,128)S(1)} %copy-done.2, f32[2,16,128]{2,1,0:T(8,128)S(1)} %copy-done.3, f32[2,16,128]{2,1,0:T(8,128)S(1)} %copy-done.4, ...), custom_call_target="tpu_custom_call" | custom-call | tf_op jit(solution)/shard_map/pallas_call | solution.py:375
  31.4 0.6 %copy.11 = f32[2,16,128]{2,1,0:T(8,128)} copy(f32[2,16,128]{2,1,0:T(8,128)S(1)} %get-tuple-element.4) | data formatting | bytes 32768
  32.1 0.6 %copy.12 = f32[2,16,128]{2,1,0:T(8,128)} copy(f32[2,16,128]{2,1,0:T(8,128)S(1)} %get-tuple-element.5) | data formatting | bytes 32768
Async XLA Ops:
  0.6 1.0 %copy-start = (f32[19,2,16,128]{3,2,1,0:T(8,128)S(1)}, f32[19,2,16,128]{3,2,1,0:T(8,128)}, u32[]{:S(2)}) copy-start(f32[19,2,16,128]{3,2,1,0:T(8,128)} %flow_ref.1) | copy-start | bytes 933892
  1.6 0.9 %copy-start.1 = (f32[7,2,16,128]{3,2,1,0:T(8,128)S(1)}, f32[7,2,16,128]{3,2,1,0:T(8,128)}, u32[]{:S(2)}) copy-start(f32[7,2,16,128]{3,2,1,0:T(8,128)} %heat_ref.1) | copy-start | bytes 344068
  2.5 0.8 %copy-start.2 = (f32[3,2,16,128]{3,2,1,0:T(8,128)S(1)}, f32[3,2,16,128]{3,2,1,0:T(8,128)}, u32[]{:S(2)}) copy-start(f32[3,2,16,128]{3,2,1,0:T(8,128)} %flow_w_ref.1) | copy-start | bytes 147460
  3.3 0.7 %copy-start.3 = (f32[2,16,128]{2,1,0:T(8,128)S(1)}, f32[2,16,128]{2,1,0:T(8,128)}, u32[]{:S(2)}) copy-start(f32[2,16,128]{2,1,0:T(8,128)} %heat_w_ref.1) | copy-start | bytes 49156
  4.0 0.7 %copy-start.4 = (f32[2,16,128]{2,1,0:T(8,128)S(1)}, f32[2,16,128]{2,1,0:T(8,128)}, u32[]{:S(2)}) copy-start(f32[2,16,128]{2,1,0:T(8,128)} %resist_ref.1) | copy-start | bytes 49156
  4.7 0.7 %copy-start.5 = (f32[2,16,128]{2,1,0:T(8,128)S(1)}, f32[2,16,128]{2,1,0:T(8,128)}, u32[]{:S(2)}) copy-start(f32[2,16,128]{2,1,0:T(8,128)} %conduct_ref.1) | copy-start | bytes 49156
  5.5 0.7 %copy-start.6 = (s32[2,16,128]{2,1,0:T(8,128)S(1)}, s32[2,16,128]{2,1,0:T(8,128)}, u32[]{:S(2)}) copy-start(s32[2,16,128]{2,1,0:T(8,128)} %solid_ref.1) | copy-start | bytes 49156

commit v2 on v1

--- a/solution.py
+++ b/solution.py
@@ -173,16 +173,24 @@
 
 
 def kernel(
-    gx, gy, flow_ref, heat_ref, flow_w_ref, heat_w_ref, resist_ref, conduct_ref, solid_ref,
-    resist_out, conduct_out,
-    ext, own_edge, edge, saved, fields, send_sem, recv_sem,
+    gx, gy, *refs
 ):
+    whole, (resist_out, conduct_out), inputs = refs[:7], refs[7:9], refs[9:16]
+    flow_ref, heat_ref, resist_ref, conduct_ref, solid_ref, flow_w_ref, heat_w_ref = inputs
+    ext, own_edge, edge, saved, fields, load_sem, send_sem, recv_sem = refs[16:]
     width, height, depth = resist_ref.shape
     sides = edge.shape[1]
     me_x, me_y = lax.axis_index("gx"), lax.axis_index("gy")
     right, left = lax.rem(me_x + 1, gx), lax.rem(me_x + gx - 1, gx)
     up, down = lax.rem(me_y + 1, gy), lax.rem(me_y + gy - 1, gy)
     columns = [(up, 0)] if sides == 1 else [(up, 0), (down, 1)]
+
+    loads = [
+        pltpu.make_async_copy(src, dst, load_sem.at[k])
+        for k, (src, dst) in enumerate(zip(whole, inputs))
+    ]
+    for load in loads:
+        load.start()
 
     barrier = pltpu.get_barrier_semaphore()
     partners = [(right, me_y), (left, me_y)]
@@ -286,6 +294,8 @@
         keep(0, x, moments)
         leave(FORWARD_0, x, collide(f, g, solid, kappa, moments))
 
+    for load in loads[:5]:
+        load.wait()
     planes(first)
     pl.semaphore_wait(barrier, len(partners))
     start(FORWARD_0)
@@ -306,6 +316,8 @@
                 members[OPPOSITE[q]] = value
         leave(SEED, x, members)
 
+    for load in loads[5:]:
+        load.wait()
     planes(seed)
     start(SEED)
 
@@ -366,30 +378,53 @@
             copy.wait_send()
 
 
+def write_out(resist_ref, conduct_ref, resist_out, conduct_out, sem):
+    stores = [
+        pltpu.make_async_copy(resist_ref, resist_out, sem.at[0]),
+        pltpu.make_async_copy(conduct_ref, conduct_out, sem.at[1]),
+    ]
+    for store in stores:
+        store.start()
+    for store in stores:
+        store.wait()
+
+
 def on_device(gx, gy, flow, heat, flow_weight, heat_weight, resistance, conductivity, solid_mask):
     shape = resistance.shape
     width, height, depth = shape
     sides = 1 if gy == 2 else 2
     count = 2 + 3 * sides
-    block = pl.BlockSpec(memory_space=pltpu.VMEM)
-    return pl.pallas_call(
+    args = (flow, heat, resistance, conductivity, solid_mask, flow_weight, heat_weight)
+    far = pl.BlockSpec(memory_space=pltpu.HBM)
+    near = pl.BlockSpec(memory_space=pltpu.VMEM)
+    result = [jax.ShapeDtypeStruct(shape, jnp.float32)] * 2
+    found = pl.pallas_call(
         functools.partial(kernel, gx, gy),
-        out_shape=[jax.ShapeDtypeStruct(shape, jnp.float32)] * 2,
-        in_specs=[block] * 7,
-        out_specs=[block] * 2,
-        scratch_shapes=[
+        out_shape=result,
+        in_specs=[far] * len(args),
+        out_specs=[near] * 2,
+        scratch_shapes=[pltpu.VMEM(a.shape, a.dtype) for a in args] + [
             pltpu.VMEM((ROUNDS, width + 2, MEMBERS, height, depth), jnp.float32),
             pltpu.VMEM((ROUNDS, width, height, depth), jnp.float32),
             pltpu.VMEM((ROUNDS, sides, width + 2, height, depth), jnp.float32),
             pltpu.VMEM((STEPS - 1, width, 15, height, depth), jnp.float32),
             pltpu.VMEM((width, 2, height, depth), jnp.float32),
+            pltpu.SemaphoreType.DMA((len(args),)),
             pltpu.SemaphoreType.DMA((ROUNDS, count)),
             pltpu.SemaphoreType.DMA((ROUNDS, count)),
         ],
         compiler_params=pltpu.CompilerParams(
-            collective_id=0, has_side_effects=True, vmem_limit_bytes=32 * 1024 * 1024
+            collective_id=0, has_side_effects=True, vmem_limit_bytes=64 * 1024 * 1024
         ),
-    )(flow, heat, flow_weight, heat_weight, resistance, conductivity, solid_mask)
+    )(*args)
+    return pl.pallas_call(
+        write_out,
+        out_shape=result,
+        in_specs=[far] * 2,
+        out_specs=[far] * 2,
+        scratch_shapes=[pltpu.SemaphoreType.DMA((2,))],
+        compiler_params=pltpu.CompilerParams(vmem_limit_bytes=64 * 1024 * 1024),
+    )(*found)
 
 
 def solution(mesh):

time: 33.2 us -> 28.9 us (0.87); the launches traced: 32.7 us -> 28.8 us
  local copies, waits for them, and re-layouts: 6.74 us -> 0 us
  Pallas kernels: 25.3 us -> 28.1 us
    unnamed x16 -> x0, local copies, waits for them, and re-layouts: 6.74 us -> none
    pallas_call x1 -> x2, Pallas kernels: 25.3 us -> 28.1 us  [the longest x1 26 us: on_device(): pl.pallas_call(functools.partial(kernel, gx, gy), out_shape=result, in_sp...]
where the time goes in v2:
time: 28.9 us; the launch traced here: 28.8 us
  Pallas kernels  28.1 us (97%)
  between operations  0.64 us (2%)
    pallas_call x1, Pallas kernels, on_device(): pl.pallas_call(functools.partial(kernel, gx, gy), out_shape=result, in_sp...  26 us
    pallas_call x1, Pallas kernels, on_device(): pl.pallas_call(write_out, out_shape=result, in_specs=[far] * 2, out_specs...  2.11 us

profile of v2, /device:TPU:0, one launch (start us, length us, event | category | flops | bytes accessed | tf_op | source)
XLA Modules:
  0.0 28.8 jit_solution(1606119143196757068)
XLA Ops:
  0.6 26.0 %shard_map.86 = (f32[2,16,128]{2,1,0:T(8,128)}, f32[2,16,128]{2,1,0:T(8,128)}) custom-call(f32[19,2,16,128]{3,2,1,0:T(8,128)} %refs_0_.1, f32[7,2,16,128]{3,2,1,0:T(8,128)} %refs_1_.1, f32[2,16,128]{2,1,0:T(8,128)} %refs_2_.1, f32[2,16,128]{2,1,0:T(8,128)} %refs_3_.1, s32[2,16,128]{2,1,0:T(8,128)} %refs_4_.1, f32[3,2,16,128]{3,2,1,0:T(8,128)} %refs_5_.1, ...), custom_call_target="tpu_custom_call" | custom-call | tf_op jit(solution)/shard_map/pallas_call | solution.py:401
  26.6 2.1 %shard_map.87 = (f32[2,16,128]{2,1,0:T(8,128)}, f32[2,16,128]{2,1,0:T(8,128)}) custom-call(f32[2,16,128]{2,1,0:T(8,128)} %get-tuple-element.4.resist_ref, f32[2,16,128]{2,1,0:T(8,128)} %get-tuple-element.5.conduct_ref), custom_call_target="tpu_custom_call" | custom-call | tf_op jit(solution)/shard_map/pallas_call | solution.py:420

commit v3 on v2

--- a/solution.py
+++ b/solution.py
@@ -201,35 +201,35 @@
 
     lane = lax.broadcasted_iota(jnp.int32, (height, depth), 1)
 
-    def copies(r):
-        made = []
-
-        def add(src, dst, device):
-            k = len(made)
-            made.append(
-                pltpu.make_async_remote_copy(
-                    src_ref=src, dst_ref=dst,
-                    send_sem=send_sem.at[r, k], recv_sem=recv_sem.at[r, k],
-                    device_id=device, device_id_type=MESH,
-                )
+    def plane(i):
+        return lax.rem(me_x + 1 + i, 2)
+
+    def copies(r, i):
+        x = plane(i)
+        upper = x == width - 1
+        beside = jnp.where(upper, right, left)
+        halo = jnp.where(upper, 0, width + 1)
+        group = pl.ds(jnp.where(upper, 0, FACE), FACE)
+
+        def remote(k, src, dst, device):
+            return pltpu.make_async_remote_copy(
+                src_ref=src, dst_ref=dst,
+                send_sem=send_sem.at[r, i, k], recv_sem=recv_sem.at[r, i, k],
+                device_id=device, device_id_type=MESH,
             )
 
+        across = [remote(0, ext.at[r, x + 1, group], ext.at[r, halo, group], (beside, me_y))]
+        within = []
         for y, side in columns:
-            add(own_edge.at[r, width - 1], edge.at[r, side, 0], (right, y))
-            add(own_edge.at[r, 0], edge.at[r, side, width + 1], (left, y))
-        add(ext.at[r, width, pl.ds(0, FACE)], ext.at[r, 0, pl.ds(0, FACE)], (right, me_y))
-        add(ext.at[r, 1, pl.ds(FACE, FACE)], ext.at[r, width + 1, pl.ds(FACE, FACE)], (left, me_y))
-        for y, side in columns:
-            add(own_edge.at[r], edge.at[r, side, pl.ds(1, width)], (me_x, y))
-        return made
-
-    def start(r):
-        for copy in copies(r):
+            k = 1 + 2 * side
+            across.append(remote(k, own_edge.at[r, x], edge.at[r, side, halo], (beside, y)))
+            within.append(remote(k + 1, own_edge.at[r, x], edge.at[r, side, x + 1], (me_x, y)))
+        return across, within
+
+    def start(r, i):
+        across, within = copies(r, i)
+        for copy in across + within:
             copy.start()
-
-    def arrive(r):
-        for copy in copies(r):
-            copy.wait_recv()
 
     def leave(r, x, members):
         packed = None
@@ -275,12 +275,24 @@
             tuple(values[4:7]), values[7], values[8] if whole else None,
         )
 
-    def planes(body):
-        def step(x, carry):
-            body(x)
+    def planes(body, after=(), then=None, early=None):
+        for r in after:
+            for i in range(2):
+                for copy in copies(r, i)[1]:
+                    copy.wait_recv()
+
+        def step(i, carry):
+            for r in after:
+                for copy in copies(r, i)[0]:
+                    copy.wait_recv()
+            if early is not None:
+                start(early, i)
+            body(plane(i))
+            if then is not None:
+                start(then, i)
             return carry
 
-        lax.fori_loop(0, width, step, 0)
+        lax.fori_loop(0, 2, step, 0)
 
     def first(x):
         solid = solid_ref[x] != 0
@@ -298,7 +310,8 @@
         load.wait()
     planes(first)
     pl.semaphore_wait(barrier, len(partners))
-    start(FORWARD_0)
+    start(FORWARD_0, 1)
+    start(FORWARD_0, 0)
 
     def seed(x):
         weights = [flow_w_ref[k, x] for k in range(3)]
@@ -319,7 +332,6 @@
     for load in loads[5:]:
         load.wait()
     planes(seed)
-    start(SEED)
 
     def second(x):
         solid, slow, kappa = solid_ref[x] != 0, fields[x, 0], fields[x, 1]
@@ -329,9 +341,7 @@
         keep(1, x, moments)
         leave(FORWARD_1, x, collide(f, g, solid, kappa, moments))
 
-    arrive(FORWARD_0)
-    planes(second)
-    start(FORWARD_1)
+    planes(second, after=(FORWARD_0,), then=FORWARD_1, early=SEED)
 
     def reverse(r, x, moments, target):
         solid, slow, kappa = solid_ref[x] != 0, fields[x, 0], fields[x, 1]
@@ -361,44 +371,29 @@
         state = [gather(FORWARD_1, x, q) for q in range(MEMBERS)]
         reverse(SEED, x, state_moments(state[:19], state[19:], fields[x, 0]), BACK_2)
 
-    arrive(SEED)
-    arrive(FORWARD_1)
-    planes(third)
-    start(BACK_2)
-
-    arrive(BACK_2)
-    planes(lambda x: reverse(BACK_2, x, kept(1, x, True), BACK_1))
-    start(BACK_1)
-
-    arrive(BACK_1)
-    planes(lambda x: reverse(BACK_1, x, kept(0, x, False), None))
+    planes(third, after=(SEED, FORWARD_1), then=BACK_2)
+    planes(
+        lambda x: reverse(BACK_2, x, kept(1, x, True), BACK_1), after=(BACK_2,), then=BACK_1
+    )
+    planes(lambda x: reverse(BACK_1, x, kept(0, x, False), None), after=(BACK_1,))
 
     for r in range(ROUNDS):
-        for copy in copies(r):
-            copy.wait_send()
-
-
-def write_out(resist_ref, conduct_ref, resist_out, conduct_out, sem):
-    stores = [
-        pltpu.make_async_copy(resist_ref, resist_out, sem.at[0]),
-        pltpu.make_async_copy(conduct_ref, conduct_out, sem.at[1]),
-    ]
-    for store in stores:
-        store.start()
-    for store in stores:
-        store.wait()
+        for i in range(2):
+            across, within = copies(r, i)
+            for copy in across + within:
+                copy.wait_send()
 
 
 def on_device(gx, gy, flow, heat, flow_weight, heat_weight, resistance, conductivity, solid_mask):
     shape = resistance.shape
     width, height, depth = shape
     sides = 1 if gy == 2 else 2
-    count = 2 + 3 * sides
+    count = 1 + 2 * sides
     args = (flow, heat, resistance, conductivity, solid_mask, flow_weight, heat_weight)
     far = pl.BlockSpec(memory_space=pltpu.HBM)
     near = pl.BlockSpec(memory_space=pltpu.VMEM)
     result = [jax.ShapeDtypeStruct(shape, jnp.float32)] * 2
-    found = pl.pallas_call(
+    return pl.pallas_call(
         functools.partial(kernel, gx, gy),
         out_shape=result,
         in_specs=[far] * len(args),
@@ -410,21 +405,13 @@
             pltpu.VMEM((STEPS - 1, width, 15, height, depth), jnp.float32),
             pltpu.VMEM((width, 2, height, depth), jnp.float32),
             pltpu.SemaphoreType.DMA((len(args),)),
-            pltpu.SemaphoreType.DMA((ROUNDS, count)),
-            pltpu.SemaphoreType.DMA((ROUNDS, count)),
+            pltpu.SemaphoreType.DMA((ROUNDS, 2, count)),
+            pltpu.SemaphoreType.DMA((ROUNDS, 2, count)),
         ],
         compiler_params=pltpu.CompilerParams(
             collective_id=0, has_side_effects=True, vmem_limit_bytes=64 * 1024 * 1024
         ),
     )(*args)
-    return pl.pallas_call(
-        write_out,
-        out_shape=result,
-        in_specs=[far] * 2,
-        out_specs=[far] * 2,
-        scratch_shapes=[pltpu.SemaphoreType.DMA((2,))],
-        compiler_params=pltpu.CompilerParams(vmem_limit_bytes=64 * 1024 * 1024),
-    )(*found)
 
 
 def solution(mesh):

time: 28.9 us -> 29.9 us (1.035)
  local copies, waits for them, and re-layouts: 0 us -> 1.94 us
  Pallas kernels: 28.1 us -> 27.1 us
    pallas_call x1 -> x0, Pallas kernels: 2.11 us -> none  [on_device(): pl.pallas_call(write_out, out_shape=result, in_specs=[far] * 2, out_specs...]
    unnamed x0 -> x4, local copies, waits for them, and re-layouts: none -> 1.94 us
    pallas_call x1, Pallas kernels: 26 us -> 27.1 us  [on_device(): pl.pallas_call(functools.partial(kernel, gx, gy), out_shape=result, in_sp...]
where the time goes in v3:
time: 29.9 us; the launch traced here: 29.7 us
  Pallas kernels  27.1 us (91%)
  local copies, waits for them, and re-layouts  1.94 us (6%)
  between operations  0.65 us (2%)
    pallas_call x1, Pallas kernels, on_device(): pl.pallas_call(functools.partial(kernel, gx, gy), out_shape=result, in_sp...  27.1 us
    unnamed x4, local copies, waits for them, and re-layouts  1.94 us

profile of v3, /device:TPU:0, one launch (start us, length us, event | category | flops | bytes accessed | tf_op | source)
XLA Modules:
  0.0 29.7 jit_solution(5356335750402145412)
XLA Ops:
  0.6 27.1 %shard_map.86 = (f32[2,16,128]{2,1,0:T(8,128)}, f32[2,16,128]{2,1,0:T(8,128)}) custom-call(f32[19,2,16,128]{3,2,1,0:T(8,128)} %refs_0_.1, f32[7,2,16,128]{3,2,1,0:T(8,128)} %refs_1_.1, f32[2,16,128]{2,1,0:T(8,128)} %refs_2_.1, f32[2,16,128]{2,1,0:T(8,128)} %refs_3_.1, s32[2,16,128]{2,1,0:T(8,128)} %refs_4_.1, f32[3,2,16,128]{3,2,1,0:T(8,128)} %refs_5_.1, ...), custom_call_target="tpu_custom_call" | custom-call | tf_op jit(solution)/shard_map/pallas_call | solution.py:396
  27.7 0.0 copy-start
  27.8 1.3 %copy.11 = f32[2,16,128]{2,1,0:T(8,128)} copy(f32[2,16,128]{2,1,0:T(8,128)} %get-tuple-element.4) | data formatting | bytes 32768
  29.1 0.0 copy-done
  29.1 0.6 %copy.12 = f32[2,16,128]{2,1,0:T(8,128)} copy(f32[2,16,128]{2,1,0:T(8,128)S(1)} %copy-done) | data formatting | bytes 32768
Async XLA Ops:
  27.7 1.3 %copy-start = (f32[2,16,128]{2,1,0:T(8,128)S(1)}, f32[2,16,128]{2,1,0:T(8,128)}, u32[]{:S(2)}) copy-start(f32[2,16,128]{2,1,0:T(8,128)} %get-tuple-element.5) | copy-start | bytes 49156

commit v4 on v3

--- a/solution.py
+++ b/solution.py
@@ -175,9 +175,10 @@
 def kernel(
     gx, gy, *refs
 ):
-    whole, (resist_out, conduct_out), inputs = refs[:7], refs[7:9], refs[9:16]
+    whole, result, inputs = refs[:7], refs[7], refs[8:15]
+    resist_out, conduct_out = result.at[0], result.at[1]
     flow_ref, heat_ref, resist_ref, conduct_ref, solid_ref, flow_w_ref, heat_w_ref = inputs
-    ext, own_edge, edge, saved, fields, load_sem, send_sem, recv_sem = refs[16:]
+    ext, own_edge, edge, saved, fields, load_sem, send_sem, recv_sem = refs[15:]
     width, height, depth = resist_ref.shape
     sides = edge.shape[1]
     me_x, me_y = lax.axis_index("gx"), lax.axis_index("gy")
@@ -281,12 +282,14 @@
                 for copy in copies(r, i)[1]:
                     copy.wait_recv()
 
+        if early is not None:
+            start(early, 1)
+            start(early, 0)
+
         def step(i, carry):
             for r in after:
                 for copy in copies(r, i)[0]:
                     copy.wait_recv()
-            if early is not None:
-                start(early, i)
             body(plane(i))
             if then is not None:
                 start(then, i)
@@ -392,12 +395,11 @@
     args = (flow, heat, resistance, conductivity, solid_mask, flow_weight, heat_weight)
     far = pl.BlockSpec(memory_space=pltpu.HBM)
     near = pl.BlockSpec(memory_space=pltpu.VMEM)
-    result = [jax.ShapeDtypeStruct(shape, jnp.float32)] * 2
-    return pl.pallas_call(
+    found = pl.pallas_call(
         functools.partial(kernel, gx, gy),
-        out_shape=result,
+        out_shape=jax.ShapeDtypeStruct((2,) + shape, jnp.float32),
         in_specs=[far] * len(args),
-        out_specs=[near] * 2,
+        out_specs=near,
         scratch_shapes=[pltpu.VMEM(a.shape, a.dtype) for a in args] + [
             pltpu.VMEM((ROUNDS, width + 2, MEMBERS, height, depth), jnp.float32),
             pltpu.VMEM((ROUNDS, width, height, depth), jnp.float32),
@@ -412,6 +414,7 @@
             collective_id=0, has_side_effects=True, vmem_limit_bytes=64 * 1024 * 1024
         ),
     )(*args)
+    return found[0], found[1]
 
 
 def solution(mesh):

time: 29.9 us -> 29 us (0.970)
  local copies, waits for them, and re-layouts: 1.94 us -> 1.35 us
  Pallas kernels: 27.1 us -> 26.8 us
    unnamed x4 -> x0, local copies, waits for them, and re-layouts: 1.94 us -> none
    squeeze x0 -> x1, local copies, waits for them, and re-layouts: none -> 1.35 us  [on_device(): return (found[0], found[1])]
    pallas_call x1, Pallas kernels: 27.1 us -> 26.8 us  [on_device(): pl.pallas_call(functools.partial(kernel, gx, gy), out_shape=jax.ShapeDtyp...]
where the time goes in v4:
time: 29 us; the launch traced here: 28.8 us
  Pallas kernels  26.8 us (92%)
  local copies, waits for them, and re-layouts  1.35 us (5%)
  between operations  0.64 us (2%)
    pallas_call x1, Pallas kernels, on_device(): pl.pallas_call(functools.partial(kernel, gx, gy), out_shape=jax.ShapeDtyp...  26.8 us
    squeeze x1, local copies, waits for them, and re-layouts, on_device(): return (found[0], found[1])  1.35 us

profile of v4, /device:TPU:0, one launch (start us, length us, event | category | flops | bytes accessed | tf_op | source)
XLA Modules:
  0.0 28.8 jit_solution(14945003148303976697)
XLA Ops:
  0.6 26.8 %shard_map.86 = f32[2,2,16,128]{3,2,1,0:T(8,128)} custom-call(f32[19,2,16,128]{3,2,1,0:T(8,128)} %refs_0_.1, f32[7,2,16,128]{3,2,1,0:T(8,128)} %refs_1_.1, f32[2,16,128]{2,1,0:T(8,128)} %refs_2_.1, f32[2,16,128]{2,1,0:T(8,128)} %refs_3_.1, s32[2,16,128]{2,1,0:T(8,128)} %refs_4_.1, f32[3,2,16,128]{3,2,1,0:T(8,128)} %refs_5_.1, f32[2,16,128]{2,1,0:T(8,128)} %refs_6_.1), custom_call_target="tpu_custom_call" | custom-call | tf_op jit(solution)/shard_map/pallas_call | solution.py:398
  27.4 1.3 %slice_bitcast_fusion = (f32[2,16,128]{2,1,0:T(8,128)}, f32[2,16,128]{2,1,0:T(8,128)}) fusion(f32[2,2,16,128]{3,2,1,0:T(8,128)} %shard_map.86), kind=kLoop, calls=%fused_computation | loop fusion | bytes 65536 | tf_op jit(solution)/shard_map/squeeze | solution.py:417

commit v5 on v4

--- a/solution.py
+++ b/solution.py
@@ -219,12 +219,14 @@
                 device_id=device, device_id_type=MESH,
             )
 
-        across = [remote(0, ext.at[r, x + 1, group], ext.at[r, halo, group], (beside, me_y))]
-        within = []
+        across, within = [], []
         for y, side in columns:
             k = 1 + 2 * side
             across.append(remote(k, own_edge.at[r, x], edge.at[r, side, halo], (beside, y)))
             within.append(remote(k + 1, own_edge.at[r, x], edge.at[r, side, x + 1], (me_x, y)))
+        across.append(
+            remote(0, ext.at[r, x + 1, group], ext.at[r, halo, group], (beside, me_y))
+        )
         return across, within
 
     def start(r, i):

time: 29 us -> 27.2 us (0.938)
  Pallas kernels: 26.8 us -> 25 us
    pallas_call x1, Pallas kernels: 26.8 us -> 25 us  [on_device(): pl.pallas_call(functools.partial(kernel, gx, gy), out_shape=jax.ShapeDtyp...]
where the time goes in v5:
time: 27.2 us; the launch traced here: 27 us
  Pallas kernels  25 us (92%)
  local copies, waits for them, and re-layouts  1.35 us (5%)
  between operations  0.64 us (2%)
    pallas_call x1, Pallas kernels, on_device(): pl.pallas_call(functools.partial(kernel, gx, gy), out_shape=jax.ShapeDtyp...  25 us
    squeeze x1, local copies, waits for them, and re-layouts, on_device(): return (found[0], found[1])  1.35 us

profile of v5, /device:TPU:0, one launch (start us, length us, event | category | flops | bytes accessed | tf_op | source)
XLA Modules:
  0.0 27.0 jit_solution(3044680828842164947)
XLA Ops:
  0.6 25.0 %shard_map.86 = f32[2,2,16,128]{3,2,1,0:T(8,128)} custom-call(f32[19,2,16,128]{3,2,1,0:T(8,128)} %refs_0_.1, f32[7,2,16,128]{3,2,1,0:T(8,128)} %refs_1_.1, f32[2,16,128]{2,1,0:T(8,128)} %refs_2_.1, f32[2,16,128]{2,1,0:T(8,128)} %refs_3_.1, s32[2,16,128]{2,1,0:T(8,128)} %refs_4_.1, f32[3,2,16,128]{3,2,1,0:T(8,128)} %refs_5_.1, f32[2,16,128]{2,1,0:T(8,128)} %refs_6_.1), custom_call_target="tpu_custom_call" | custom-call | tf_op jit(solution)/shard_map/pallas_call | solution.py:400
  25.6 1.3 %slice_bitcast_fusion = (f32[2,16,128]{2,1,0:T(8,128)}, f32[2,16,128]{2,1,0:T(8,128)}) fusion(f32[2,2,16,128]{3,2,1,0:T(8,128)} %shard_map.86), kind=kLoop, calls=%fused_computation | loop fusion | bytes 65536 | tf_op jit(solution)/shard_map/squeeze | solution.py:419

commit v6 on v5

--- a/solution.py
+++ b/solution.py
@@ -30,6 +30,7 @@
 UP = [q for q in range(MEMBERS) if VELOCITY[q][1] == 1]
 DOWN = [q for q in range(MEMBERS) if VELOCITY[q][1] == -1]
 ROUNDS = 5
+PARTS = 3
 FORWARD_0, SEED, FORWARD_1, BACK_2, BACK_1 = range(ROUNDS)
 MESH = pl.DeviceIdType.MESH
 
@@ -190,15 +191,14 @@
         pltpu.make_async_copy(src, dst, load_sem.at[k])
         for k, (src, dst) in enumerate(zip(whole, inputs))
     ]
-    for load in loads:
-        load.start()
-
     barrier = pltpu.get_barrier_semaphore()
     partners = [(right, me_y), (left, me_y)]
     for y, _ in columns:
         partners += [(me_x, y), (right, y), (left, y)]
     for partner in partners:
         pl.semaphore_signal(barrier, inc=1, device_id=partner, device_id_type=MESH)
+    for load in loads:
+        load.start()
 
     lane = lax.broadcasted_iota(jnp.int32, (height, depth), 1)
 
@@ -210,7 +210,7 @@
         upper = x == width - 1
         beside = jnp.where(upper, right, left)
         halo = jnp.where(upper, 0, width + 1)
-        group = pl.ds(jnp.where(upper, 0, FACE), FACE)
+        group = jnp.where(upper, 0, FACE)
 
         def remote(k, src, dst, device):
             return pltpu.make_async_remote_copy(
@@ -221,12 +221,14 @@
 
         across, within = [], []
         for y, side in columns:
-            k = 1 + 2 * side
+            k = PARTS + 2 * side
             across.append(remote(k, own_edge.at[r, x], edge.at[r, side, halo], (beside, y)))
             within.append(remote(k + 1, own_edge.at[r, x], edge.at[r, side, x + 1], (me_x, y)))
-        across.append(
-            remote(0, ext.at[r, x + 1, group], ext.at[r, halo, group], (beside, me_y))
-        )
+        for k in range(PARTS):
+            part = pl.ds(group + k * (FACE // PARTS), FACE // PARTS)
+            across.append(
+                remote(k, ext.at[r, x + 1, part], ext.at[r, halo, part], (beside, me_y))
+            )
         return across, within
 
     def start(r, i):
@@ -313,9 +315,10 @@
 
     for load in loads[:5]:
         load.wait()
-    planes(first)
+    first(plane(1))
     pl.semaphore_wait(barrier, len(partners))
     start(FORWARD_0, 1)
+    first(plane(0))
     start(FORWARD_0, 0)
 
     def seed(x):
@@ -393,7 +396,7 @@
     shape = resistance.shape
     width, height, depth = shape
     sides = 1 if gy == 2 else 2
-    count = 1 + 2 * sides
+    count = PARTS + 2 * sides
     args = (flow, heat, resistance, conductivity, solid_mask, flow_weight, heat_weight)
     far = pl.BlockSpec(memory_space=pltpu.HBM)
     near = pl.BlockSpec(memory_space=pltpu.VMEM)

time: 27.2 us -> 27.6 us (1.015)
  Pallas kernels: 25 us -> 25.4 us
    pallas_call x1, Pallas kernels: 25 us -> 25.4 us  [on_device(): pl.pallas_call(functools.partial(kernel, gx, gy), out_shape=jax.ShapeDtyp...]
where the time goes in v6:
time: 27.6 us; the launch traced here: 27.4 us
  Pallas kernels  25.4 us (92%)
  local copies, waits for them, and re-layouts  1.35 us (5%)
  between operations  0.64 us (2%)
    pallas_call x1, Pallas kernels, on_device(): pl.pallas_call(functools.partial(kernel, gx, gy), out_shape=jax.ShapeDtyp...  25.4 us
    squeeze x1, local copies, waits for them, and re-layouts, on_device(): return (found[0], found[1])  1.35 us

profile of v6, /device:TPU:0, one launch (start us, length us, event | category | flops | bytes accessed | tf_op | source)
XLA Modules:
  0.0 27.4 jit_solution(13631918406206265902)
XLA Ops:
  0.6 25.4 %shard_map.86 = f32[2,2,16,128]{3,2,1,0:T(8,128)} custom-call(f32[19,2,16,128]{3,2,1,0:T(8,128)} %refs_0_.1, f32[7,2,16,128]{3,2,1,0:T(8,128)} %refs_1_.1, f32[2,16,128]{2,1,0:T(8,128)} %refs_2_.1, f32[2,16,128]{2,1,0:T(8,128)} %refs_3_.1, s32[2,16,128]{2,1,0:T(8,128)} %refs_4_.1, f32[3,2,16,128]{3,2,1,0:T(8,128)} %refs_5_.1, f32[2,16,128]{2,1,0:T(8,128)} %refs_6_.1), custom_call_target="tpu_custom_call" | custom-call | tf_op jit(solution)/shard_map/pallas_call | solution.py:403
  26.0 1.3 %slice_bitcast_fusion = (f32[2,16,128]{2,1,0:T(8,128)}, f32[2,16,128]{2,1,0:T(8,128)}) fusion(f32[2,2,16,128]{3,2,1,0:T(8,128)} %shard_map.86), kind=kLoop, calls=%fused_computation | loop fusion | bytes 65536 | tf_op jit(solution)/shard_map/squeeze | solution.py:422

commit v7 on v6

--- a/solution.py
+++ b/solution.py
@@ -30,7 +30,7 @@
 UP = [q for q in range(MEMBERS) if VELOCITY[q][1] == 1]
 DOWN = [q for q in range(MEMBERS) if VELOCITY[q][1] == -1]
 ROUNDS = 5
-PARTS = 3
+PARTS = 1
 FORWARD_0, SEED, FORWARD_1, BACK_2, BACK_1 = range(ROUNDS)
 MESH = pl.DeviceIdType.MESH
 
@@ -179,7 +179,7 @@
     whole, result, inputs = refs[:7], refs[7], refs[8:15]
     resist_out, conduct_out = result.at[0], result.at[1]
     flow_ref, heat_ref, resist_ref, conduct_ref, solid_ref, flow_w_ref, heat_w_ref = inputs
-    ext, own_edge, edge, saved, fields, load_sem, send_sem, recv_sem = refs[15:]
+    ext, corner, own_edge, edge, saved, fields, load_sem, send_sem, recv_sem = refs[15:]
     width, height, depth = resist_ref.shape
     sides = edge.shape[1]
     me_x, me_y = lax.axis_index("gx"), lax.axis_index("gy")
@@ -222,7 +222,7 @@
         across, within = [], []
         for y, side in columns:
             k = PARTS + 2 * side
-            across.append(remote(k, own_edge.at[r, x], edge.at[r, side, halo], (beside, y)))
+            across.append(remote(k, corner.at[r, x], edge.at[r, side, halo], (beside, y)))
             within.append(remote(k + 1, own_edge.at[r, x], edge.at[r, side, x + 1], (me_x, y)))
         for k in range(PARTS):
             part = pl.ds(group + k * (FACE // PARTS), FACE // PARTS)
@@ -231,30 +231,39 @@
             )
         return across, within
 
-    def start(r, i):
-        across, within = copies(r, i)
-        for copy in across + within:
+    def start(r, i, which):
+        for copy in copies(r, i)[which]:
             copy.start()
 
-    def leave(r, x, members):
+    def leave(r, x, members, send=None, entry=False):
         packed = None
-        for q in range(MEMBERS):
-            if members[q] is None:
-                continue
-            value = members[q]
-            _, step_y, step_z = VELOCITY[q]
-            if step_z:
-                value = pltpu.roll(value, step_z % height, 0)
-            if step_y:
-                value = pltpu.roll(value, step_y % depth, 1)
-            ext[r, x + 1, SLOT[q]] = value
-            if step_y:
-                place = UP.index(q) if step_y == 1 else DOWN.index(q)
-                shift = place * step_y % depth
-                where = place if step_y == 1 else depth - 1 - place
-                turned = pltpu.roll(value, shift, 1) if shift else value
-                packed = turned if packed is None else jnp.where(lane == where, turned, packed)
-        own_edge[r, x] = packed
+        for crossing in (True, False):
+            for q in range(MEMBERS):
+                step_x, step_y, step_z = VELOCITY[q]
+                if members[q] is None or bool(step_x) != crossing:
+                    continue
+                value = members[q]
+                if step_z:
+                    value = pltpu.roll(value, step_z % height, 0)
+                if step_y:
+                    value = pltpu.roll(value, step_y % depth, 1)
+                ext[r, x + 1, SLOT[q]] = value
+                if step_y:
+                    place = UP.index(q) if step_y == 1 else DOWN.index(q)
+                    shift = place * step_y % depth
+                    where = place if step_y == 1 else depth - 1 - place
+                    turned = pltpu.roll(value, shift, 1) if shift else value
+                    packed = turned if packed is None else jnp.where(lane == where, turned, packed)
+            if crossing:
+                corner[r, x] = packed
+                if entry:
+                    pl.semaphore_wait(barrier, len(partners))
+                if send is not None:
+                    start(r, send, 0)
+            else:
+                own_edge[r, x] = packed
+                if send is not None:
+                    start(r, send, 1)
 
     def gather(r, x, q):
         step_x, step_y, _ = VELOCITY[q]
@@ -280,28 +289,27 @@
             tuple(values[4:7]), values[7], values[8] if whole else None,
         )
 
-    def planes(body, after=(), then=None, early=None):
+    def planes(body, after=(), early=None):
         for r in after:
             for i in range(2):
                 for copy in copies(r, i)[1]:
                     copy.wait_recv()
 
         if early is not None:
-            start(early, 1)
-            start(early, 0)
+            for i in (1, 0):
+                for which in range(2):
+                    start(early, i, which)
 
         def step(i, carry):
             for r in after:
                 for copy in copies(r, i)[0]:
                     copy.wait_recv()
-            body(plane(i))
-            if then is not None:
-                start(then, i)
+            body(plane(i), i)
             return carry
 
         lax.fori_loop(0, 2, step, 0)
 
-    def first(x):
+    def first(x, i):
         solid = solid_ref[x] != 0
         slow = jnp.where(solid, 0.0, 1.0) / (1.0 + resist_ref[x])
         kappa = 1.0 / (0.5 + 0.4 * conduct_ref[x])
@@ -311,17 +319,14 @@
         g = [heat_ref[q, x] for q in range(7)]
         moments = state_moments(f, g, slow)
         keep(0, x, moments)
-        leave(FORWARD_0, x, collide(f, g, solid, kappa, moments))
+        leave(FORWARD_0, x, collide(f, g, solid, kappa, moments), i, entry=i == 1)
 
     for load in loads[:5]:
         load.wait()
-    first(plane(1))
-    pl.semaphore_wait(barrier, len(partners))
-    start(FORWARD_0, 1)
-    first(plane(0))
-    start(FORWARD_0, 0)
-
-    def seed(x):
+    first(plane(1), 1)
+    first(plane(0), 0)
+
+    def seed(x, _):
         weights = [flow_w_ref[k, x] for k in range(3)]
         heat = heat_w_ref[x]
         members = [None] * MEMBERS
@@ -341,17 +346,17 @@
         load.wait()
     planes(seed)
 
-    def second(x):
+    def second(x, i):
         solid, slow, kappa = solid_ref[x] != 0, fields[x, 0], fields[x, 1]
         state = [gather(FORWARD_0, x, q) for q in range(MEMBERS)]
         f, g = state[:19], state[19:]
         moments = state_moments(f, g, slow)
         keep(1, x, moments)
-        leave(FORWARD_1, x, collide(f, g, solid, kappa, moments))
-
-    planes(second, after=(FORWARD_0,), then=FORWARD_1, early=SEED)
-
-    def reverse(r, x, moments, target):
+        leave(FORWARD_1, x, collide(f, g, solid, kappa, moments), i)
+
+    planes(second, after=(FORWARD_0,), early=SEED)
+
+    def reverse(r, x, i, moments, target):
         solid, slow, kappa = solid_ref[x] != 0, fields[x, 0], fields[x, 1]
         back = [
             jnp.zeros((height, depth), jnp.float32) if r == SEED and q == 0
@@ -373,17 +378,15 @@
             conduct_out[x] = (conduct_out[x] + conduct) * (-0.4 * kappa * kappa)
         if target is not None:
             out = collide_back(l, m, sums, moments, u_back, bent, solid, slow, kappa)
-            leave(target, x, [out[OPPOSITE[q]] for q in range(MEMBERS)])
-
-    def third(x):
+            leave(target, x, [out[OPPOSITE[q]] for q in range(MEMBERS)], i)
+
+    def third(x, i):
         state = [gather(FORWARD_1, x, q) for q in range(MEMBERS)]
-        reverse(SEED, x, state_moments(state[:19], state[19:], fields[x, 0]), BACK_2)
-
-    planes(third, after=(SEED, FORWARD_1), then=BACK_2)
-    planes(
-        lambda x: reverse(BACK_2, x, kept(1, x, True), BACK_1), after=(BACK_2,), then=BACK_1
-    )
-    planes(lambda x: reverse(BACK_1, x, kept(0, x, False), None), after=(BACK_1,))
+        reverse(SEED, x, i, state_moments(state[:19], state[19:], fields[x, 0]), BACK_2)
+
+    planes(third, after=(SEED, FORWARD_1))
+    planes(lambda x, i: reverse(BACK_2, x, i, kept(1, x, True), BACK_1), after=(BACK_2,))
+    planes(lambda x, i: reverse(BACK_1, x, i, kept(0, x, False), None), after=(BACK_1,))
 
     for r in range(ROUNDS):
         for i in range(2):
@@ -408,6 +411,7 @@
         scratch_shapes=[pltpu.VMEM(a.shape, a.dtype) for a in args] + [
             pltpu.VMEM((ROUNDS, width + 2, MEMBERS, height, depth), jnp.float32),
             pltpu.VMEM((ROUNDS, width, height, depth), jnp.float32),
+            pltpu.VMEM((ROUNDS, width, height, depth), jnp.float32),
             pltpu.VMEM((ROUNDS, sides, width + 2, height, depth), jnp.float32),
             pltpu.VMEM((STEPS - 1, width, 15, height, depth), jnp.float32),
             pltpu.VMEM((width, 2, height, depth), jnp.float32),

time: 27.6 us -> 27.2 us (0.986)
  Pallas kernels: 25.4 us -> 24.9 us
    pallas_call x1, Pallas kernels: 25.4 us -> 24.9 us  [on_device(): pl.pallas_call(functools.partial(kernel, gx, gy), out_shape=jax.ShapeDtyp...]
where the time goes in v7:
time: 27.2 us; the launch traced here: 26.9 us
  Pallas kernels  24.9 us (92%)
  local copies, waits for them, and re-layouts  1.35 us (5%)
  between operations  0.64 us (2%)
    pallas_call x1, Pallas kernels, on_device(): pl.pallas_call(functools.partial(kernel, gx, gy), out_shape=jax.ShapeDtyp...  24.9 us
    squeeze x1, local copies, waits for them, and re-layouts, on_device(): return (found[0], found[1])  1.35 us

profile of v7, /device:TPU:0, one launch (start us, length us, event | category | flops | bytes accessed | tf_op | source)
XLA Modules:
  0.0 26.9 jit_solution(3055894053854259962)
XLA Ops:
  0.6 24.9 %shard_map.86 = f32[2,2,16,128]{3,2,1,0:T(8,128)} custom-call(f32[19,2,16,128]{3,2,1,0:T(8,128)} %refs_0_.1, f32[7,2,16,128]{3,2,1,0:T(8,128)} %refs_1_.1, f32[2,16,128]{2,1,0:T(8,128)} %refs_2_.1, f32[2,16,128]{2,1,0:T(8,128)} %refs_3_.1, s32[2,16,128]{2,1,0:T(8,128)} %refs_4_.1, f32[3,2,16,128]{3,2,1,0:T(8,128)} %refs_5_.1, f32[2,16,128]{2,1,0:T(8,128)} %refs_6_.1), custom_call_target="tpu_custom_call" | custom-call | tf_op jit(solution)/shard_map/pallas_call | solution.py:406
  25.6 1.3 %slice_bitcast_fusion = (f32[2,16,128]{2,1,0:T(8,128)}, f32[2,16,128]{2,1,0:T(8,128)}) fusion(f32[2,2,16,128]{3,2,1,0:T(8,128)} %shard_map.86), kind=kLoop, calls=%fused_computation | loop fusion | bytes 65536 | tf_op jit(solution)/shard_map/squeeze | solution.py:426
